TPU v7x, 32 devices: a whole 2x2x4 slice. The times are simulated.
32 devices in a mesh: grp: 2 (over x), ctx: 16 (over z, y, core).
Axes of the slice: x: 2, y: 2, z: 4, core: 2. Of those that a mesh axis runs over, the one named last changes fastest.
Arguments:
- queries: bfloat16 [4, 12, 64, 128], P(None, 'grp'), parts along dimension 1, may hold values from -150 to 150
- key_cache: bfloat16 [12, 8, 2048, 128], P('grp', None, 'ctx'), parts along dimension 0, may hold values from -6 to 6
- value_cache: bfloat16 [12, 8, 2048, 128], P('grp', None, 'ctx'), parts along dimension 0, may hold values from -6 to 6
- row_lengths: int32 [12], P('grp'), parts along dimension 0, may hold values from 128 to 2048, as said below
- kept_tiles: int32 [4, 12, 16], P(None, 'grp'), parts along dimension 1, may hold values from 0 to 1, as said below
- tile_dest: int32 [12, 8, 16], P('grp'), parts along dimension 0, may hold values from 0 to 15, as said below
Outputs:
- attn_out: bfloat16 [4, 12, 64, 128], P(None, 'grp'), parts along dimension 1
- tile_mass: float32 [12, 8, 16], P('grp', None, 'ctx'), parts along dimension 0
- moved_keys: bfloat16 [12, 8, 2048, 128], P('grp', None, 'ctx'), parts along dimension 0
- moved_values: bfloat16 [12, 8, 2048, 128], P('grp', None, 'ctx'), parts along dimension 0
There are 2 independent parts, one for each index of `grp`. A program takes and returns all parts, laid end to end along the dimension named above; each array names one. Nothing has to cross between parts.
Inputs may be any that keep to these rules, and one draw needn't show every extreme that they name: `row_lengths`: at least 128 positions of every row are filled; some row is filled to all 2048 positions. `kept_tiles`: A tile dropped at one step stays dropped at all later steps; tile 0 of every row is kept at every step. For each row and head, tile_dest is a permutation of the 16 tiles. The 1 tiles that one index of ctx holds for a row and head all go, in some order, to the index a per-row-and-head offset further along ctx, wrapping around; that offset is the same for every index. No offset is used by more than 3 row-head pairs, and some offset is used by exactly 3. The offsets 16 // 2 and 1 are used by some row-head pair in every draw.
All inputs are finite; a program needn't handle non-finite values.
Results may differ from a plain program's by a relative error of at most 0.0027.
Values may be sent and summed in bfloat16 or wider, within the bound.
No kernel may reach another device: no remote copies, remote signals or barrier semaphores. Data moves between devices by JAX's collectives and lax.ppermute only.
A program may use at most 64 MiB of HBM per device.

v0:
```python
import functools

import jax
import jax.numpy as jnp
from jax import lax
from jax.experimental import pallas as pl
from jax.experimental.pallas import tpu as pltpu
from jax.sharding import PartitionSpec as P

absent_score = -1e30
LANES = 128
FIELD = 32
F32 = jnp.float32
BF16 = jnp.bfloat16
VMEM = pl.BlockSpec(memory_space=pltpu.VMEM)
SMEM = pl.BlockSpec(memory_space=pltpu.SMEM)
HBM = pl.BlockSpec(memory_space=pltpu.HBM)
ANY = pl.BlockSpec(memory_space=pl.ANY)
PARAMS = pltpu.CompilerParams(vmem_limit_bytes=16 * 1024 * 1024)
WHOLE = pltpu.CompilerParams(vmem_limit_bytes=62 * 1024 * 1024)


COST = pl.CostEstimate(flops=1000, bytes_accessed=1000, transcendentals=0)


def stage_kernel(devices, group, me_ref, dest_hbm, k_ref, buf, table, k_vm, dest, counts, sem, load_sem):
    rows, heads = k_ref.shape[:2]
    small = pltpu.make_async_copy(dest_hbm, dest, sem.at[0])
    small.start()
    loads = []
    for row in range(rows):
        copy = pltpu.make_async_copy(k_ref.at[row], k_vm.at[row], load_sem.at[row])
        copy.start()
        loads.append(copy)
    me = me_ref[0]

    def clear(i, carry):
        counts[i] = 0
        for k in range(group):
            table[i * group + k] = -1
        return carry

    lax.fori_loop(0, devices, clear, 0)
    small.wait()
    for row in range(rows):
        loads[row].wait()

        def send(head, carry):
            offset = lax.rem(dest[row, head, 0], devices)
            rank = jnp.minimum(counts[offset], group - 1)
            counts[offset] = rank + 1
            table[offset * group + rank] = row * heads + head
            slot = lax.rem(me + offset, devices) * group + rank
            pltpu.make_async_copy(k_vm.at[row, head], buf.at[slot], sem.at[1]).start()
            return carry

        lax.fori_loop(0, heads, send, 0)
    pltpu.make_async_copy(k_ref, k_vm, sem.at[1]).wait()


def attend_kernel(
    devices, group, levels,
    me_ref, table, len_hbm, kept_hbm, q_hbm, k_ref, v_ref,
    stats_ref, *rest,
):
    chunks, bufs = rest[:levels // 2], rest[levels // 2:levels // 2 + devices - 1]
    q_vm, k_vm, v_vm, work, len_ref, kept_ref, load_sem, small_sem, out_sem, buf_sem = rest[levels // 2 + devices - 1:]
    rows, heads, tile, width = k_ref.shape
    steps, _, q_heads, _ = q_hbm.shape
    per = q_heads // heads
    me = me_ref[0]

    small = [
        pltpu.make_async_copy(len_hbm, len_ref, small_sem.at[0]),
        pltpu.make_async_copy(kept_hbm, kept_ref, small_sem.at[1]),
    ]
    for copy in small:
        copy.start()
    loads = []
    for row in range(rows):
        copies = [
            pltpu.make_async_copy(q_hbm.at[:, row], q_vm.at[row], load_sem.at[0, row]),
            pltpu.make_async_copy(k_ref.at[row], k_vm.at[row], load_sem.at[1, row]),
            pltpu.make_async_copy(v_ref.at[row], v_vm.at[row], load_sem.at[2, row]),
        ]
        for copy in copies:
            copy.start()
        loads.append(copies)
    for copy in small:
        copy.wait()

    lane = lax.broadcasted_iota(jnp.int32, (per, tile), 1)
    pair_lane = lax.broadcasted_iota(jnp.int32, (steps * per, LANES), 1)
    peaks = jnp.full((steps * per, LANES), absent_score, F32)
    totals = jnp.zeros((steps * per, LANES), F32)
    order = [jnp.bitwise_xor(place_of(me), level) for level in range(levels)]
    scale = width ** -0.5
    block = steps * per
    for row in range(rows):
        for copy in loads[row]:
            copy.wait()
        queries = [q_vm[row, step].astype(F32) for step in order]
        live = []
        for step in order:
            limit = jnp.where(kept_ref[row, step, me] > 0, len_ref[row] - me * tile, 0)
            live.append(lane < limit)
        live = jnp.concatenate(live * heads, axis=0)
        scores = []
        for head in range(heads):
            q = jnp.concatenate([x[head * per:(head + 1) * per] for x in queries], axis=0).astype(BF16)
            scores.append(lax.dot_general(
                q, k_vm[row, head], (((1,), (1,)), ((), ())), preferred_element_type=F32
            ))
        scores = jnp.concatenate(scores, axis=0) * scale
        peak = jnp.max(jnp.where(live, scores, absent_score), axis=1, keepdims=True)
        weights = jnp.where(live, jnp.exp(scores - peak), 0.0)
        total = jnp.sum(weights, axis=1, keepdims=True)
        rounded = weights.astype(BF16)
        for head in range(heads):
            out = jnp.dot(
                rounded[head * block:(head + 1) * block], v_vm[row, head], preferred_element_type=F32
            )
            pair = row * heads + head
            for i in range(levels):
                work[i, pair * per:(pair + 1) * per, :] = out[i * per:(i + 1) * per]
            here = pair_lane == pair
            peaks = jnp.where(here, peak[head * block:(head + 1) * block], peaks)
            totals = jnp.where(here, total[head * block:(head + 1) * block], totals)
    base = rows * q_heads
    for i in range(levels):
        work[i, base:base + per, :] = peaks[i * per:(i + 1) * per]
        work[i, base + per:base + 2 * per, :] = totals[i * per:(i + 1) * per]
    stats_ref[0] = peaks
    stats_ref[1] = totals
    copies = [
        pltpu.make_async_copy(work.at[pl.ds(2 * i, 2)], chunks[i], out_sem.at[i]) for i in range(levels // 2)
    ]
    for copy in copies:
        copy.start()
    for offset in range(1, devices):
        for k in range(group):
            pair = jnp.maximum(table[offset * group + k], 0)
            src = v_vm.at[pair // heads, lax.rem(pair, heads)]
            pltpu.make_async_copy(src, bufs[offset - 1].at[k], buf_sem.at[offset - 1]).start()
        copies.append(pltpu.make_async_copy(bufs[offset - 1], bufs[offset - 1], buf_sem.at[offset - 1]))
    for copy in copies:
        copy.wait()


def place_of(me):
    return lax.rem(me, 2) * 2 + lax.rem(me // 2, 2)


def merge(refs, first, base, pairs, per):
    peaks = [ref[base:base + per, :] for ref in refs]
    totals = [ref[base + per:base + 2 * per, :] for ref in refs]
    peak = functools.reduce(jnp.maximum, peaks)
    factors = [jnp.exp(x - peak) for x in peaks]
    total = functools.reduce(jnp.add, [f * t for f, t in zip(factors, totals)])

    def summed(pair):
        at = first + pair * per
        return functools.reduce(jnp.add, [
            jnp.broadcast_to(f[:, pair:pair + 1], (per, ref.shape[1])) * ref[at:at + per, :]
            for f, ref in zip(factors, refs)
        ])

    return peak, total, summed


def core_kernel(pairs, per, own_ref, got_ref, *outs):
    work, sem = outs[-2:]
    base = pairs * per
    for i in range(2):
        peak, total, summed = merge([own_ref.at[i], got_ref.at[i]], 0, base, pairs, per)
        for pair in range(pairs):
            work[i, pair * per:(pair + 1) * per, :] = summed(pair)
        work[i, base:base + per, :] = peak
        work[i, base + per:base + 2 * per, :] = total
    copies = [pltpu.make_async_copy(work.at[i], outs[i], sem.at[i]) for i in range(2)]
    for copy in copies:
        copy.start()
    for copy in copies:
        copy.wait()


def near_kernel(pairs, per, levels, parts, me_ref, *refs):
    ins, outs, (work, sem) = refs[:2], refs[2:2 + parts], refs[2 + parts:]
    share = pairs // parts
    base = share * per
    peak, total, summed = merge(ins, 0, pairs * per, pairs, per)
    for part in range(parts):
        for i in range(share):
            work[part, i * per:(i + 1) * per, :] = summed(part * share + i)
        shift = (LANES - part * share) % LANES
        work[part, base:base + per, :] = pltpu.roll(peak, shift, 1) if shift else peak
        work[part, base + per:base + 2 * per, :] = pltpu.roll(total, shift, 1) if shift else total
    mine = me_ref[0] // levels
    copies = [
        pltpu.make_async_copy(work.at[jnp.bitwise_xor(mine, part)], outs[part], sem.at[part])
        for part in range(parts)
    ]
    for copy in copies:
        copy.start()
    for copy in copies:
        copy.wait()


def far_kernel(share, per, parts, *refs):
    ins, (out, work, sem) = refs[:parts], refs[parts:]
    peak, total, summed = merge(ins, 0, share * per, share, per)
    lane = lax.broadcasted_iota(jnp.int32, peak.shape, 1)
    total = jnp.where(lane < share, total, 1.0)
    peak = jnp.where(lane < share, peak, 0.0)

    def result(pair):
        return summed(pair) / jnp.broadcast_to(total[:, pair:pair + 1], (per, LANES))

    for pair in range(0, share, 2):
        both = jnp.concatenate([result(pair), result(pair + 1)], axis=0)
        work[pair * per:(pair + 2) * per, :] = both.astype(BF16)
    rest = jnp.concatenate([peak, total], axis=0)
    lane = lax.broadcasted_iota(jnp.int32, rest.shape, 1)
    packed = jnp.zeros_like(rest)
    for i in range(3):
        part = rest.astype(BF16).astype(F32)
        rest = rest - part
        here = (lane >= i * FIELD) & (lane < (i + 1) * FIELD)
        packed = jnp.where(here, pltpu.roll(part, i * FIELD, 1) if i else part, packed)
    work[share * per:(share + 2) * per, :] = packed.astype(BF16)
    copy = pltpu.make_async_copy(work, out, sem)
    copy.start()
    copy.wait()


def join_kernel(levels, parts, me_ref, *refs):
    ins, (out, sem) = refs[:parts], refs[parts:]
    mine = me_ref[0] // levels
    copies = [
        pltpu.make_async_copy(ins[part], out.at[jnp.bitwise_xor(mine, part)], sem.at[part])
        for part in range(parts)
    ]
    for copy in copies:
        copy.start()
    for copy in copies:
        copy.wait()


def finish_kernel(pairs, share, per, heads, levels, parts, me_ref, stats_ref, *refs):
    ins, out, mass_ref = refs[:levels], refs[levels], refs[levels + 1]
    base = share * per
    lane = lax.broadcasted_iota(jnp.int32, (per, LANES), 1)
    mass = jnp.zeros((per, LANES), F32)
    for level in range(levels):
        step = jnp.bitwise_xor(place_of(me_ref[0]), level)
        peak = jnp.zeros((per, LANES), F32)
        total = jnp.ones((per, LANES), F32)
        for part in range(parts):
            start = part * share
            out[step, part * base:(part + 1) * base, :] = ins[level][part, :base, :]
            packed = ins[level][part, base:base + 2 * per, :].astype(F32)
            fields = [pltpu.roll(packed, (start - field * FIELD) % LANES, 1) for field in (2, 1)]
            fields.append(pltpu.roll(packed, start, 1) if start else packed)
            both = functools.reduce(jnp.add, fields)
            here = (lane >= start) & (lane < start + share)
            peak = jnp.where(here, both[:per], peak)
            total = jnp.where(here, both[per:], total)
        at = level * per
        coefficient = jnp.exp(jnp.minimum(stats_ref[0, at:at + per, :] - peak, 0.0)) / total
        mass = mass + stats_ref[1, at:at + per, :] * coefficient
    mass = jnp.sum(mass, axis=0, keepdims=True)
    for row in range(pairs // heads):
        mass_ref[row] = mass[:, row * heads:(row + 1) * heads]


def place_keys_kernel(devices, group, me_ref, table, got_ref, k_ref, got_vm, sem, load_sem):
    heads = k_ref.shape[1]
    me = me_ref[0]
    loads = []
    for offset in range(devices):
        source = lax.rem(me + devices - offset, devices)
        part = got_ref.at[pl.ds(source * group, group)]
        copy = pltpu.make_async_copy(part, got_vm.at[pl.ds(offset * group, group)], load_sem.at[offset])
        copy.start()
        loads.append(copy)
    for offset in range(devices):
        loads[offset].wait()
        put(table, offset, group, heads, got_vm, k_ref, sem)
    pltpu.make_async_copy(k_ref, k_ref, sem).wait()


def place_values_kernel(devices, group, table, own_ref, *refs):
    got, (v_ref, got_vm, sem, load_sem) = refs[:devices - 1], refs[devices - 1:]
    heads = v_ref.shape[1]
    loads = []
    for offset in range(devices):
        if offset:
            copies = [pltpu.make_async_copy(
                got[offset - 1], got_vm.at[pl.ds(offset * group, group)], load_sem.at[offset]
            )]
        else:
            copies = []
            for k in range(group):
                pair = jnp.maximum(table[k], 0)
                src = own_ref.at[pair // heads, lax.rem(pair, heads)]
                copies.append(pltpu.make_async_copy(src, got_vm.at[k], load_sem.at[devices + k]))
        for copy in copies:
            copy.start()
        loads.append(copies)
    for offset in range(devices):
        for copy in loads[offset]:
            copy.wait()
        put(table, offset, group, heads, got_vm, v_ref, sem)
    pltpu.make_async_copy(v_ref, v_ref, sem).wait()


def put(table, offset, group, heads, got_vm, ref, sem):
    for slot in range(offset * group, (offset + 1) * group):
        pair = table[slot]

        @pl.when(pair >= 0)
        def _():
            dst = ref.at[pair // heads, lax.rem(pair, heads)]
            pltpu.make_async_copy(got_vm.at[slot], dst, sem).start()


def local(queries, key_cache, value_cache, row_lengths, kept_tiles, tile_dest):
    devices = lax.axis_size("ctx")
    rows, heads, span, width = key_cache.shape
    steps, _, q_heads, _ = queries.shape
    per = q_heads // heads
    pairs = rows * heads
    group = -(-pairs // devices)
    levels = 4
    parts = devices // levels
    two_level = devices == levels * parts and parts & (parts - 1) == 0 and pairs % (2 * parts) == 0
    share = pairs // parts
    two_level = two_level and share <= FIELD and pairs <= LANES
    assert steps == levels and tile_dest.shape[2] == devices

    me = lax.axis_index("ctx").astype(jnp.int32).reshape(1)
    kept = jnp.transpose(kept_tiles, (1, 0, 2))
    chunk_rows = rows * q_heads + 2 * per
    buf_type = jax.ShapeDtypeStruct((group, span, width), BF16)

    keys_out, table = pl.pallas_call(
        functools.partial(stage_kernel, devices, group),
        out_shape=[
            jax.ShapeDtypeStruct((devices * group, span, width), BF16),
            jax.ShapeDtypeStruct((devices * group,), jnp.int32),
        ],
        in_specs=[SMEM, HBM, HBM],
        out_specs=[HBM, SMEM],
        scratch_shapes=[
            pltpu.VMEM(key_cache.shape, BF16),
            pltpu.SMEM(tile_dest.shape, jnp.int32),
            pltpu.SMEM((devices,), jnp.int32),
            pltpu.SemaphoreType.DMA((2,)),
            pltpu.SemaphoreType.DMA((rows,)),
        ],
        compiler_params=WHOLE,
        cost_estimate=COST,
        name="stage",
    )(me, tile_dest, key_cache)
    keys_in = lax.all_to_all(keys_out, "ctx", split_axis=0, concat_axis=0, tiled=True)

    stats, *outs = pl.pallas_call(
        functools.partial(attend_kernel, devices, group, levels),
        out_shape=[
            jax.ShapeDtypeStruct((2, steps * per, LANES), F32),
        ] + [jax.ShapeDtypeStruct((2, chunk_rows, width), F32)] * 2 + [buf_type] * (devices - 1),
        in_specs=[SMEM, SMEM, HBM, HBM, HBM, HBM, HBM],
        out_specs=[VMEM] + [HBM] * (devices + 1),
        scratch_shapes=[
            pltpu.VMEM((rows, steps, q_heads, width), BF16),
            pltpu.VMEM(key_cache.shape, BF16),
            pltpu.VMEM(value_cache.shape, BF16),
            pltpu.VMEM((levels, chunk_rows, width), F32),
            pltpu.SMEM(row_lengths.shape, jnp.int32),
            pltpu.SMEM(kept.shape, jnp.int32),
            pltpu.SemaphoreType.DMA((3, rows)),
            pltpu.SemaphoreType.DMA((2,)),
            pltpu.SemaphoreType.DMA((2,)),
            pltpu.SemaphoreType.DMA((devices - 1,)),
        ],
        compiler_params=WHOLE,
        cost_estimate=COST,
        name="attend",
    )(me, table, row_lengths, kept, queries, key_cache, value_cache)
    chunks, bufs = outs[:2], outs[2:]
    values_in = [
        lax.ppermute(bufs[offset - 1], "ctx", [(i, (i + offset) % devices) for i in range(devices)])
        for offset in range(1, devices)
    ]

    if two_level:
        def flip(x, bits):
            return lax.ppermute(x, "ctx", [(i, i ^ bits) for i in range(devices)])

        part_rows = share * per + 2 * per
        block_type = jax.ShapeDtypeStruct((chunk_rows, width), F32)
        kept_block, sent_block = pl.pallas_call(
            functools.partial(core_kernel, pairs, per),
            out_shape=[block_type] * 2,
            in_specs=[VMEM, VMEM],
            out_specs=[HBM, HBM],
            scratch_shapes=[pltpu.VMEM((2, chunk_rows, width), F32), pltpu.SemaphoreType.DMA((2,))],
            compiler_params=WHOLE,
            cost_estimate=COST,
            name="core",
        )(chunks[0], flip(chunks[1], 1))
        pieces = pl.pallas_call(
            functools.partial(near_kernel, pairs, per, levels, parts),
            out_shape=[jax.ShapeDtypeStruct((part_rows, width), F32)] * parts,
            in_specs=[SMEM, VMEM, VMEM],
            out_specs=[HBM] * parts,
            scratch_shapes=[pltpu.VMEM((parts, part_rows, width), F32), pltpu.SemaphoreType.DMA((parts,))],
            compiler_params=WHOLE,
            cost_estimate=COST,
            name="near",
        )(me, kept_block, flip(sent_block, 2))
        message = pl.pallas_call(
            functools.partial(far_kernel, share, per, parts),
            out_shape=jax.ShapeDtypeStruct((part_rows, width), BF16),
            in_specs=[VMEM] * parts,
            out_specs=HBM,
            scratch_shapes=[pltpu.VMEM((part_rows, width), BF16), pltpu.SemaphoreType.DMA],
            compiler_params=WHOLE,
            cost_estimate=COST,
            name="far",
        )(pieces[0], *[flip(pieces[i], levels * i) for i in range(1, parts)])
        joined = pl.pallas_call(
            functools.partial(join_kernel, levels, parts),
            out_shape=jax.ShapeDtypeStruct((parts, part_rows, width), BF16),
            in_specs=[SMEM] + [VMEM] * parts,
            out_specs=HBM,
            scratch_shapes=[pltpu.SemaphoreType.DMA((parts,))],
            compiler_params=WHOLE,
            cost_estimate=COST,
            name="join",
        )(me, message, *[flip(message, levels * i) for i in range(1, parts)])
        other = flip(joined, 2)
        attn_out, mass = pl.pallas_call(
            functools.partial(finish_kernel, pairs, share, per, heads, levels, parts),
            out_shape=[
                jax.ShapeDtypeStruct((steps, rows * q_heads, width), BF16),
                jax.ShapeDtypeStruct((rows, 1, heads), F32),
            ],
            in_specs=[SMEM, VMEM] + [VMEM] * levels,
            out_specs=[VMEM, VMEM],
            compiler_params=PARAMS,
            cost_estimate=COST,
            name="finish",
        )(me, stats, joined, other, flip(joined, 1), flip(other, 1))
        attn_out = attn_out.reshape(queries.shape)
        tile_mass = jnp.transpose(mass, (0, 2, 1))
    else:
        order = jnp.bitwise_xor(place_of(me[0]), jnp.arange(levels))
        stacked = jnp.concatenate(chunks)[:, :rows * q_heads][order].reshape(steps, rows, heads, per, width)

        def by_pair(x):
            x = x.reshape(levels, per, LANES)[order][:, :, :pairs].reshape(steps, per, rows, heads)
            return jnp.transpose(x, (0, 2, 3, 1))

        peak, total = by_pair(stats[0]), by_pair(stats[1])
        factor = jnp.exp(peak - lax.pmax(peak, "ctx"))
        denominator, summed = lax.psum((total * factor, stacked * factor[..., None]), "ctx")
        attn_out = (summed / denominator[..., None]).astype(BF16).reshape(queries.shape)
        tile_mass = jnp.sum(total * factor / denominator, axis=(0, 3))[:, :, None]

    moved_keys = pl.pallas_call(
        functools.partial(place_keys_kernel, devices, group),
        out_shape=jax.ShapeDtypeStruct(key_cache.shape, BF16),
        in_specs=[SMEM, SMEM, HBM],
        out_specs=HBM,
        scratch_shapes=[
            pltpu.VMEM(keys_in.shape, BF16),
            pltpu.SemaphoreType.DMA,
            pltpu.SemaphoreType.DMA((devices,)),
        ],
        compiler_params=WHOLE,
        cost_estimate=COST,
        name="place_keys",
    )(me, table, keys_in)
    moved_values = pl.pallas_call(
        functools.partial(place_values_kernel, devices, group),
        out_shape=jax.ShapeDtypeStruct(value_cache.shape, BF16),
        in_specs=[SMEM] + [HBM] * devices,
        out_specs=HBM,
        scratch_shapes=[
            pltpu.VMEM(keys_in.shape, BF16),
            pltpu.SemaphoreType.DMA,
            pltpu.SemaphoreType.DMA((devices + group,)),
        ],
        compiler_params=WHOLE,
        cost_estimate=COST,
        name="place_values",
    )(table, value_cache, *values_in)
    return attn_out, tile_mass, moved_keys, moved_values


def solution(mesh):
    in_specs = (
        P(None, "grp", None, None),
        P("grp", None, "ctx", None),
        P("grp", None, "ctx", None),
        P("grp"),
        P(None, "grp", None),
        P("grp", None, None),
    )
    out_specs = (
        P(None, "grp", None, None),
        P("grp", None, "ctx"),
        P("grp", None, "ctx", None),
        P("grp", None, "ctx", None),
    )
    return jax.shard_map(local, mesh=mesh, in_specs=in_specs, out_specs=out_specs, check_vma=False)
```

profile of v0, /device:TPU:0, one launch (start us, length us, event | category | flops | bytes accessed | tf_op | source)
XLA Modules:
  0.0 108.6 jit_solution(4416680636004527247)
XLA Ops:
  0.6 3.1 %stage.1 = (bf16[48,128,128]{2,1,0:T(8,128)(2,1)}, s32[48]{0:T(128)}) custom-call(s32[1]{0:T(128)} %bitcast.me_ref, s32[6,8,16]{2,1,0:T(8,128)} %dest_hbm.1, bf16[6,8,128,128]{3,2,1,0:T(8,128)(2,1)} %k_ref.3), custom_call_target="tpu_custom_call" | custom-call | flops 1000 | bytes 1000 | tf_op jit(solution)/shard_map/stage/pallas_call | solution.py:346
  3.8 7.4 %all-to-all-start = ((bf16[48,128,128]{2,1,0:T(8,128)(2,1)}), bf16[48,128,128]{2,1,0:T(8,128)(2,1)}, u32[]{:S(2)}, u32[]{:S(2)}) async-start(bf16[48,128,128]{2,1,0:T(8,128)(2,1)} %get-tuple-element.44), calls=%async_computation | async-start | bytes 3145728 | tf_op jit(solution)/shard_map/all_to_all | solution.py:365
  11.2 6.5 %attend.1 = (f32[2,32,128]{2,1,0:T(8,128)}, f32[2,400,128]{2,1,0:T(8,128)}, f32[2,400,128]{2,1,0:T(8,128)}, bf16[3,128,128]{2,1,0:T(8,128)(2,1)}, bf16[3,128,128...) custom-call(s32[1]{0:T(128)} %bitcast.me_ref, ...), custom_call_target="tpu_custom_call" | custom-call | flops 1000 | bytes 1000 | tf_op jit(solution)/shard_map/attend/pallas_call | solution.py:367
  17.7 0.4 collective-permute-start
  18.1 1.6 %collective-permute-done.got_ref = f32[2,400,128]{2,1,0:T(8,128)S(1)} collective-permute-done((f32[2,400,128]{2,1,0:T(8,128)}, f32[2,400,128]{2,1,0:T(8,128)S(1)}, u32[]{:S(2)}, u32[]{:S(2)}) %collective-permute-start) | collective-permute-done | bytes 409632 | tf_op jit(solution)/shard_map/ppermute | solution.py:398
  19.8 0.8 copy-done.2
  20.5 2.3 %core.1 = (f32[400,128]{1,0:T(8,128)}, f32[400,128]{1,0:T(8,128)}) custom-call(f32[2,400,128]{2,1,0:T(8,128)} %get-tuple-element.34.own_ref, f32[2,400,128]{2,1,0:T(8,128)} %copy-done.2), custom_call_target="tpu_custom_call" | custom-call | flops 1000 | bytes 1000 | tf_op jit(solution)/shard_map/core/pallas_call | solution.py:402
  22.8 1.9 %collective-permute-start.1 = (f32[400,128]{1,0:T(8,128)}, f32[400,128]{1,0:T(8,128)S(1)}, u32[]{:S(2)}, u32[]{:S(2)}) collective-permute-start(f32[400,128]{1,0:T(8,128)} %get-tuple-element.37), channel_id=1, source_target_pairs={{0,2},{1,3},{2,0},{3,1},{4,6},{5,7},{6,4},{7,5},{8,10},{9,11},{10,... | collective-permute-start | bytes 614408 | tf_op jit(solution)/shard_map/ppermute | solution.py:398
  24.7 10.9 %collective-permute-done.1.refs_1_ = f32[400,128]{1,0:T(8,128)S(1)} collective-permute-done((f32[400,128]{1,0:T(8,128)}, f32[400,128]{1,0:T(8,128)S(1)}, u32[]{:S(2)}, u32[]{:S(2)}) %collective-permute-start.1) | collective-permute-done | bytes 204832 | tf_op jit(solution)/shard_map/ppermute | solution.py:398
  35.6 0.7 copy-done.3
  36.3 2.0 %near.1 = (f32[112,128]{1,0:T(8,128)}, f32[112,128]{1,0:T(8,128)}, f32[112,128]{1,0:T(8,128)}, f32[112,128]{1,0:T(8,128)}) custom-call(s32[1]{0:T(128)} %bitcast.me_ref, f32[400,128]{1,0:T(8,128)} %get-tuple-element.36.refs_0_, f32[400,128]{1,0:T(8,128)} %copy-done.3), custom_call_target="tpu_custom_call" | custom-call | flops 1000 | bytes 1000 | tf_op jit(solution)/shard_map/near/pallas_call | solution.py:412
  38.3 0.5 collective-permute-start.2
  38.8 0.0 collective-permute-start.11
  38.8 2.1 %collective-permute-start.12 = (bf16[3,128,128]{2,1,0:T(8,128)(2,1)}, bf16[3,128,128]{2,1,0:T(8,128)(2,1)S(1)}, u32[]{:S(2)}, u32[]{:S(2)}) collective-permute-start(bf16[3,128,128]{2,1,0:T(8,128)(2,1)} %get-tuple-element.46), channel_id=1, source_target_pairs={{0,2},{1,3},{2,4},{3,5},{4,6},{5,7},{6,8},{7,9},{8,10},{9,11},{10,... | collective-permute-start | bytes 294920 | tf_op jit(solution)/shard_map/ppermute | solution.py:392
  40.9 2.8 %collective-permute-start.13 = (bf16[3,128,128]{2,1,0:T(8,128)(2,1)}, bf16[3,128,128]{2,1,0:T(8,128)(2,1)S(1)}, u32[]{:S(2)}, u32[]{:S(2)}) collective-permute-start(bf16[3,128,128]{2,1,0:T(8,128)(2,1)} %get-tuple-element.47), channel_id=1, source_target_pairs={{0,3},{1,4},{2,5},{3,6},{4,7},{5,8},{6,9},{7,10},{8,11},{9,12},{10... | collective-permute-start | bytes 294920 | tf_op jit(solution)/shard_map/ppermute | solution.py:392
  43.7 2.8 %collective-permute-done.2.refs_1_ = f32[112,128]{1,0:T(8,128)S(1)} collective-permute-done((f32[112,128]{1,0:T(8,128)}, f32[112,128]{1,0:T(8,128)S(1)}, u32[]{:S(2)}, u32[]{:S(2)}) %collective-permute-start.2) | collective-permute-done | bytes 57376 | tf_op jit(solution)/shard_map/ppermute | solution.py:398
  46.5 7.8 %collective-permute-done.3.refs_2_ = f32[112,128]{1,0:T(8,128)S(1)} collective-permute-done((f32[112,128]{1,0:T(8,128)}, f32[112,128]{1,0:T(8,128)S(1)}, u32[]{:S(2)}, u32[]{:S(2)}) %collective-permute-start.3) | collective-permute-done | bytes 57376 | tf_op jit(solution)/shard_map/ppermute | solution.py:398
  54.3 0.6 copy-done.20
  54.9 0.0 copy-done.21
  54.9 1.7 %far.1.refs_0_ = bf16[112,128]{1,0:T(8,128)(2,1)} custom-call(f32[112,128]{1,0:T(8,128)} %get-tuple-element.38.refs_0_, f32[112,128]{1,0:T(8,128)} %copy-done.19, f32[112,128]{1,0:T(8,128)} %copy-done.20, f32[112,128]{1,0:T(8,128)} %copy-done.21), custom_call_target="tpu_custom_call" | custom-call | flops 1000 | bytes 1000 | tf_op jit(solution)/shard_map/far/pallas_call | solution.py:422
  56.6 1.4 %collective-permute-start.5 = (bf16[112,128]{1,0:T(8,128)(2,1)}, bf16[112,128]{1,0:T(8,128)(2,1)S(1)}, u32[]{:S(2)}, u32[]{:S(2)}) collective-permute-start(bf16[112,128]{1,0:T(8,128)(2,1)} %far.1.refs_0_), channel_id=1, source_target_pairs={{0,4},{1,5},{2,6},{3,7},{4,0},{5,1},{6,2},{7,3},{8,12},{9,13},{10,... | collective-permute-start | bytes 86024 | tf_op jit(solution)/shard_map/ppermute | solution.py:398
  58.0 3.1 %collective-permute-start.6 = (bf16[112,128]{1,0:T(8,128)(2,1)}, bf16[112,128]{1,0:T(8,128)(2,1)S(1)}, u32[]{:S(2)}, u32[]{:S(2)}) collective-permute-start(bf16[112,128]{1,0:T(8,128)(2,1)} %far.1.refs_0_), channel_id=1, source_target_pairs={{0,8},{1,9},{2,10},{3,11},{4,12},{5,13},{6,14},{7,15},{8,0},{9,1},... | collective-permute-start | bytes 86024 | tf_op jit(solution)/shard_map/ppermute | solution.py:398
  61.0 0.0 collective-permute-start.7
  61.1 0.1 collective-permute-start.15
  61.1 0.2 collective-permute-done.5.refs_1_
  61.3 5.9 %collective-permute-start.16 = (bf16[3,128,128]{2,1,0:T(8,128)(2,1)}, bf16[3,128,128]{2,1,0:T(8,128)(2,1)S(1)}, u32[]{:S(2)}, u32[]{:S(2)}) collective-permute-start(bf16[3,128,128]{2,1,0:T(8,128)(2,1)} %get-tuple-element.50), channel_id=1, source_target_pairs={{0,6},{1,7},{2,8},{3,9},{4,10},{5,11},{6,12},{7,13},{8,14},{9,15},... | collective-permute-start | bytes 294920 | tf_op jit(solution)/shard_map/ppermute | solution.py:392
  67.2 3.8 %collective-permute-start.17 = (bf16[3,128,128]{2,1,0:T(8,128)(2,1)}, bf16[3,128,128]{2,1,0:T(8,128)(2,1)S(1)}, u32[]{:S(2)}, u32[]{:S(2)}) collective-permute-start(bf16[3,128,128]{2,1,0:T(8,128)(2,1)} %get-tuple-element.51), channel_id=1, source_target_pairs={{0,7},{1,8},{2,9},{3,10},{4,11},{5,12},{6,13},{7,14},{8,15},{9,0},... | collective-permute-start | bytes 294920 | tf_op jit(solution)/shard_map/ppermute | solution.py:392
  71.1 0.6 collective-permute-start.18
  71.7 0.0 copy-done.24
  71.7 1.5 %join.1.refs_0_ = bf16[4,112,128]{2,1,0:T(8,128)(2,1)} custom-call(s32[1]{0:T(128)} %bitcast.me_ref, bf16[112,128]{1,0:T(8,128)(2,1)} %far.1.refs_0_, bf16[112,128]{1,0:T(8,128)(2,1)} %copy-done.22, bf16[112,128]{1,0:T(8,128)(2,1)} %copy-done.23, bf16[112,128]{1,0:T(8,128)(2,1)} %copy-done.24), custom_call_target="tpu_custom_call" | custom-call | flops 1000 | bytes 1000 | tf_op jit(solution)/shard_map/join/pallas_call | solution.py:432
  73.2 1.8 %collective-permute-start.8 = (bf16[4,112,128]{2,1,0:T(8,128)(2,1)}, bf16[4,112,128]{2,1,0:T(8,128)(2,1)S(1)}, u32[]{:S(2)}, u32[]{:S(2)}) collective-permute-start(bf16[4,112,128]{2,1,0:T(8,128)(2,1)} %join.1.refs_0_), channel_id=1, source_target_pairs={{0,2},{1,3},{2,0},{3,1},{4,6},{5,7},{6,4},{7,5},{8,10},{9,11},{10,... | collective-permute-start | bytes 344072 | tf_op jit(solution)/shard_map/ppermute | solution.py:398
  75.0 0.7 collective-permute-start.19
  75.6 4.2 %collective-permute-done.16.refs_5_ = bf16[3,128,128]{2,1,0:T(8,128)(2,1)S(1)} collective-permute-done((bf16[3,128,128]{2,1,0:T(8,128)(2,1)}, bf16[3,128,128]{2,1,0:T(8,128)(2,1)S(1)}, u32[]{:S(2)}, u32[]{:S(2)}) %collective-permute-start.16) | collective-permute-done | bytes 98336 | tf_op jit(solution)/shard_map/ppermute | solution.py:392
  79.9 1.9 %collective-permute-done.17.refs_6_ = bf16[3,128,128]{2,1,0:T(8,128)(2,1)S(1)} collective-permute-done((bf16[3,128,128]{2,1,0:T(8,128)(2,1)}, bf16[3,128,128]{2,1,0:T(8,128)(2,1)S(1)}, u32[]{:S(2)}, u32[]{:S(2)}) %collective-permute-start.17) | collective-permute-done | bytes 98336 | tf_op jit(solution)/shard_map/ppermute | solution.py:392
  81.8 2.2 %collective-permute-start.21 = (bf16[3,128,128]{2,1,0:T(8,128)(2,1)S(1)}, bf16[3,128,128]{2,1,0:T(8,128)(2,1)S(1)}, u32[]{:S(2)}, u32[]{:S(2)}) collective-permute-start(bf16[3,128,128]{2,1,0:T(8,128)(2,1)S(1)} %copy-done.26), channel_id=1, source_target_pairs={{0,11},{1,12},{2,13},{3,14},{4,15},{5,0},{6,1},{7,2},{8,3},{9,4},{... | collective-permute-start | bytes 294920 | tf_op jit(solution)/shard_map/ppermute | solution.py:392
  84.0 3.1 %collective-permute-start.22 = (bf16[3,128,128]{2,1,0:T(8,128)(2,1)S(1)}, bf16[3,128,128]{2,1,0:T(8,128)(2,1)S(1)}, u32[]{:S(2)}, u32[]{:S(2)}) collective-permute-start(bf16[3,128,128]{2,1,0:T(8,128)(2,1)S(1)} %copy-done.25), channel_id=1, source_target_pairs={{0,12},{1,13},{2,14},{3,15},{4,0},{5,1},{6,2},{7,3},{8,4},{9,5},{1... | collective-permute-start | bytes 294920 | tf_op jit(solution)/shard_map/ppermute | solution.py:392
  87.1 0.2 collective-permute-start.9
  87.3 0.3 collective-permute-start.10
  87.6 1.4 %collective-permute-done.20.refs_9_ = bf16[3,128,128]{2,1,0:T(8,128)(2,1)S(1)} collective-permute-done((bf16[3,128,128]{2,1,0:T(8,128)(2,1)S(1)}, bf16[3,128,128]{2,1,0:T(8,128)(2,1)S(1)}, u32[]{:S(2)}, u32[]{:S(2)}) %collective-permute-start.20) | collective-permute-done | bytes 98336 | tf_op jit(solution)/shard_map/ppermute | solution.py:392
  89.0 1.4 %collective-permute-start.23 = (bf16[3,128,128]{2,1,0:T(8,128)(2,1)}, bf16[3,128,128]{2,1,0:T(8,128)(2,1)S(1)}, u32[]{:S(2)}, u32[]{:S(2)}) collective-permute-start(bf16[3,128,128]{2,1,0:T(8,128)(2,1)} %get-tuple-element.57), channel_id=1, source_target_pairs={{0,13},{1,14},{2,15},{3,0},{4,1},{5,2},{6,3},{7,4},{8,5},{9,6},{10... | collective-permute-start | bytes 294920 | tf_op jit(solution)/shard_map/ppermute | solution.py:392
  90.4 5.6 %collective-permute-start.24 = (bf16[3,128,128]{2,1,0:T(8,128)(2,1)}, bf16[3,128,128]{2,1,0:T(8,128)(2,1)S(1)}, u32[]{:S(2)}, u32[]{:S(2)}) collective-permute-start(bf16[3,128,128]{2,1,0:T(8,128)(2,1)} %get-tuple-element.58), channel_id=1, source_target_pairs={{0,14},{1,15},{2,0},{3,1},{4,2},{5,3},{6,4},{7,5},{8,6},{9,7},{10,... | collective-permute-start | bytes 294920 | tf_op jit(solution)/shard_map/ppermute | solution.py:392
  96.1 1.5 %collective-permute-start.25 = (bf16[3,128,128]{2,1,0:T(8,128)(2,1)}, bf16[3,128,128]{2,1,0:T(8,128)(2,1)S(1)}, u32[]{:S(2)}, u32[]{:S(2)}) collective-permute-start(bf16[3,128,128]{2,1,0:T(8,128)(2,1)} %get-tuple-element.59), channel_id=1, source_target_pairs={{0,15},{1,0},{2,1},{3,2},{4,3},{5,4},{6,5},{7,6},{8,7},{9,8},{10,9... | collective-permute-start | bytes 294920 | tf_op jit(solution)/shard_map/ppermute | solution.py:392
  97.6 1.9 %collective-permute-done.24.refs_13_ = bf16[3,128,128]{2,1,0:T(8,128)(2,1)S(1)} collective-permute-done((bf16[3,128,128]{2,1,0:T(8,128)(2,1)}, bf16[3,128,128]{2,1,0:T(8,128)(2,1)S(1)}, u32[]{:S(2)}, u32[]{:S(2)}) %collective-permute-start.24) | collective-permute-done | bytes 98336 | tf_op jit(solution)/shard_map/ppermute | solution.py:392
  99.5 1.5 %collective-permute-done.25.refs_14_ = bf16[3,128,128]{2,1,0:T(8,128)(2,1)S(1)} collective-permute-done((bf16[3,128,128]{2,1,0:T(8,128)(2,1)}, bf16[3,128,128]{2,1,0:T(8,128)(2,1)S(1)}, u32[]{:S(2)}, u32[]{:S(2)}) %collective-permute-start.25) | collective-permute-done | bytes 98336 | tf_op jit(solution)/shard_map/ppermute | solution.py:392
  101.1 0.6 copy-done.18
  101.8 3.0 %place_values.1 = bf16[6,8,128,128]{3,2,1,0:T(8,128)(2,1)} custom-call(s32[48]{0:T(128)} %get-tuple-element.32.table, bf16[6,8,128,128]{3,2,1,0:T(8,128)(2,1)} %own_ref.1, bf16[3,128,128]{2,1,0:T(8,128)(2,1)} %copy-done.4, bf16[3,128,128]{2,1,0:T(8,128)(2,1)} %copy-done.5, bf16[3,128,128]{2,1,0:T(8,128)(2,1)} %copy-done.6, bf16[3,128,128]{2,1,0:T(8,128)(2,1)} %copy-done.7, ...), custom_call_target="tpu_custom_call" | custom-call | flops 1000 | bytes 1000 | tf_op jit(solution)/shard_map/place_values/pallas_call | solution.py:485
  104.8 0.9 finish.1
  105.7 2.9 %place_keys.1 = bf16[6,8,128,128]{3,2,1,0:T(8,128)(2,1)} custom-call(s32[1]{0:T(128)} %bitcast.me_ref, s32[48]{0:T(128)} %get-tuple-element.32.table, bf16[48,128,128]{2,1,0:T(8,128)(2,1)} %all-to-all-done.got_ref), custom_call_target="tpu_custom_call" | custom-call | flops 1000 | bytes 1000 | tf_op jit(solution)/shard_map/place_keys/pallas_call | solution.py:471
  (73 shorter events, 0.2 us)
Async XLA Ops:
  3.8 101.9 %all-to-all-start = ((bf16[48,128,128]{2,1,0:T(8,128)(2,1)}), bf16[48,128,128]{2,1,0:T(8,128)(2,1)}, u32[]{:S(2)}, u32[]{:S(2)}) async-start(bf16[48,128,128]{2,1,0:T(8,128)(2,1)} %get-tuple-element.44), calls=%async_computation | async-start | bytes 3145728 | tf_op jit(solution)/shard_map/all_to_all | solution.py:365
  17.7 57.3 %copy-start.28 = (bf16[3,128,128]{2,1,0:T(8,128)(2,1)S(1)}, bf16[3,128,128]{2,1,0:T(8,128)(2,1)}, u32[]{:S(2)}) copy-start(bf16[3,128,128]{2,1,0:T(8,128)(2,1)} %get-tuple-element.53) | copy-start | bytes 294916
  17.7 62.2 %copy-start.27 = (bf16[3,128,128]{2,1,0:T(8,128)(2,1)S(1)}, bf16[3,128,128]{2,1,0:T(8,128)(2,1)}, u32[]{:S(2)}) copy-start(bf16[3,128,128]{2,1,0:T(8,128)(2,1)} %get-tuple-element.54) | copy-start | bytes 294916
  17.7 64.0 %copy-start.26 = (bf16[3,128,128]{2,1,0:T(8,128)(2,1)S(1)}, bf16[3,128,128]{2,1,0:T(8,128)(2,1)}, u32[]{:S(2)}) copy-start(bf16[3,128,128]{2,1,0:T(8,128)(2,1)} %get-tuple-element.55) | copy-start | bytes 294916
  17.7 66.3 %copy-start.25 = (bf16[3,128,128]{2,1,0:T(8,128)(2,1)S(1)}, bf16[3,128,128]{2,1,0:T(8,128)(2,1)}, u32[]{:S(2)}) copy-start(bf16[3,128,128]{2,1,0:T(8,128)(2,1)} %get-tuple-element.56) | copy-start | bytes 294916
  17.7 2.0 %collective-permute-start = (f32[2,400,128]{2,1,0:T(8,128)}, f32[2,400,128]{2,1,0:T(8,128)S(1)}, u32[]{:S(2)}, u32[]{:S(2)}) collective-permute-start(f32[2,400,128]{2,1,0:T(8,128)} %get-tuple-element.35), channel_id=1, source_target_pairs={{0,1},{1,0},{2,3},{3,2},{4,5},{5,4},{6,7},{7,6},{8,9},{9,8},{10,11... | collective-permute-start | bytes 1228808 | tf_op jit(solution)/shard_map/ppermute | solution.py:398
  22.8 12.8 %collective-permute-start.1 = (f32[400,128]{1,0:T(8,128)}, f32[400,128]{1,0:T(8,128)S(1)}, u32[]{:S(2)}, u32[]{:S(2)}) collective-permute-start(f32[400,128]{1,0:T(8,128)} %get-tuple-element.37), channel_id=1, source_target_pairs={{0,2},{1,3},{2,0},{3,1},{4,6},{5,7},{6,4},{7,5},{8,10},{9,11},{10,... | collective-permute-start | bytes 614408 | tf_op jit(solution)/shard_map/ppermute | solution.py:398
  38.3 8.2 %collective-permute-start.2 = (f32[112,128]{1,0:T(8,128)}, f32[112,128]{1,0:T(8,128)S(1)}, u32[]{:S(2)}, u32[]{:S(2)}) collective-permute-start(f32[112,128]{1,0:T(8,128)} %get-tuple-element.39), channel_id=1, source_target_pairs={{0,4},{1,5},{2,6},{3,7},{4,0},{5,1},{6,2},{7,3},{8,12},{9,13},{10,... | collective-permute-start | bytes 172040 | tf_op jit(solution)/shard_map/ppermute | solution.py:398
  38.8 19.1 %collective-permute-start.11 = (bf16[3,128,128]{2,1,0:T(8,128)(2,1)}, bf16[3,128,128]{2,1,0:T(8,128)(2,1)S(1)}, u32[]{:S(2)}, u32[]{:S(2)}) collective-permute-start(bf16[3,128,128]{2,1,0:T(8,128)(2,1)} %get-tuple-element.45), channel_id=1, source_target_pairs={{0,1},{1,2},{2,3},{3,4},{4,5},{5,6},{6,7},{7,8},{8,9},{9,10},{10,1... | collective-permute-start | bytes 294920 | tf_op jit(solution)/shard_map/ppermute | solution.py:392
  38.8 22.2 %collective-permute-start.12 = (bf16[3,128,128]{2,1,0:T(8,128)(2,1)}, bf16[3,128,128]{2,1,0:T(8,128)(2,1)S(1)}, u32[]{:S(2)}, u32[]{:S(2)}) collective-permute-start(bf16[3,128,128]{2,1,0:T(8,128)(2,1)} %get-tuple-element.46), channel_id=1, source_target_pairs={{0,2},{1,3},{2,4},{3,5},{4,6},{5,7},{6,8},{7,9},{8,10},{9,11},{10,... | collective-permute-start | bytes 294920 | tf_op jit(solution)/shard_map/ppermute | solution.py:392
  40.9 20.2 %collective-permute-start.13 = (bf16[3,128,128]{2,1,0:T(8,128)(2,1)}, bf16[3,128,128]{2,1,0:T(8,128)(2,1)S(1)}, u32[]{:S(2)}, u32[]{:S(2)}) collective-permute-start(bf16[3,128,128]{2,1,0:T(8,128)(2,1)} %get-tuple-element.47), channel_id=1, source_target_pairs={{0,3},{1,4},{2,5},{3,6},{4,7},{5,8},{6,9},{7,10},{8,11},{9,12},{10... | collective-permute-start | bytes 294920 | tf_op jit(solution)/shard_map/ppermute | solution.py:392
  43.7 10.6 %collective-permute-start.3 = (f32[112,128]{1,0:T(8,128)}, f32[112,128]{1,0:T(8,128)S(1)}, u32[]{:S(2)}, u32[]{:S(2)}) collective-permute-start(f32[112,128]{1,0:T(8,128)} %get-tuple-element.40), channel_id=1, source_target_pairs={{0,8},{1,9},{2,10},{3,11},{4,12},{5,13},{6,14},{7,15},{8,0},{9,1},... | collective-permute-start | bytes 172040 | tf_op jit(solution)/shard_map/ppermute | solution.py:398
  46.5 7.8 %copy-start.19 = (f32[112,128]{1,0:T(8,128)}, f32[112,128]{1,0:T(8,128)S(1)}, u32[]{:S(2)}) copy-start(f32[112,128]{1,0:T(8,128)S(1)} %collective-permute-done.2.refs_1_) | copy-start | bytes 172036
  46.5 7.8 %collective-permute-start.4 = (f32[112,128]{1,0:T(8,128)}, f32[112,128]{1,0:T(8,128)S(1)}, u32[]{:S(2)}, u32[]{:S(2)}) collective-permute-start(f32[112,128]{1,0:T(8,128)} %get-tuple-element.41), channel_id=1, source_target_pairs={{0,12},{1,13},{2,14},{3,15},{4,8},{5,9},{6,10},{7,11},{8,4},{9,5},... | collective-permute-start | bytes 172040 | tf_op jit(solution)/shard_map/ppermute | solution.py:398
  54.3 18.9 %collective-permute-start.14 = (bf16[3,128,128]{2,1,0:T(8,128)(2,1)}, bf16[3,128,128]{2,1,0:T(8,128)(2,1)S(1)}, u32[]{:S(2)}, u32[]{:S(2)}) collective-permute-start(bf16[3,128,128]{2,1,0:T(8,128)(2,1)} %get-tuple-element.48), channel_id=1, source_target_pairs={{0,4},{1,5},{2,6},{3,7},{4,8},{5,9},{6,10},{7,11},{8,12},{9,13},{1... | collective-permute-start | bytes 294920 | tf_op jit(solution)/shard_map/ppermute | solution.py:392
  56.6 4.7 %collective-permute-start.5 = (bf16[112,128]{1,0:T(8,128)(2,1)}, bf16[112,128]{1,0:T(8,128)(2,1)S(1)}, u32[]{:S(2)}, u32[]{:S(2)}) collective-permute-start(bf16[112,128]{1,0:T(8,128)(2,1)} %far.1.refs_0_), channel_id=1, source_target_pairs={{0,4},{1,5},{2,6},{3,7},{4,0},{5,1},{6,2},{7,3},{8,12},{9,13},{10,... | collective-permute-start | bytes 86024 | tf_op jit(solution)/shard_map/ppermute | solution.py:398
  58.0 43.1 %copy-start.4 = (bf16[3,128,128]{2,1,0:T(8,128)(2,1)}, bf16[3,128,128]{2,1,0:T(8,128)(2,1)S(1)}, u32[]{:S(2)}) copy-start(bf16[3,128,128]{2,1,0:T(8,128)(2,1)S(1)} %collective-permute-done.11.refs_0_) | copy-start | bytes 294916
  58.0 9.3 %collective-permute-start.6 = (bf16[112,128]{1,0:T(8,128)(2,1)}, bf16[112,128]{1,0:T(8,128)(2,1)S(1)}, u32[]{:S(2)}, u32[]{:S(2)}) collective-permute-start(bf16[112,128]{1,0:T(8,128)(2,1)} %far.1.refs_0_), channel_id=1, source_target_pairs={{0,8},{1,9},{2,10},{3,11},{4,12},{5,13},{6,14},{7,15},{8,0},{9,1},... | collective-permute-start | bytes 86024 | tf_op jit(solution)/shard_map/ppermute | solution.py:398
  61.0 40.0 %copy-start.5 = (bf16[3,128,128]{2,1,0:T(8,128)(2,1)}, bf16[3,128,128]{2,1,0:T(8,128)(2,1)S(1)}, u32[]{:S(2)}) copy-start(bf16[3,128,128]{2,1,0:T(8,128)(2,1)S(1)} %collective-permute-done.12.refs_1_) | copy-start | bytes 294916
  61.0 10.0 %collective-permute-start.7 = (bf16[112,128]{1,0:T(8,128)(2,1)}, bf16[112,128]{1,0:T(8,128)(2,1)S(1)}, u32[]{:S(2)}, u32[]{:S(2)}) collective-permute-start(bf16[112,128]{1,0:T(8,128)(2,1)} %far.1.refs_0_), channel_id=1, source_target_pairs={{0,12},{1,13},{2,14},{3,15},{4,8},{5,9},{6,10},{7,11},{8,4},{9,5},... | collective-permute-start | bytes 86024 | tf_op jit(solution)/shard_map/ppermute | solution.py:398
  61.0 40.0 %copy-start.6 = (bf16[3,128,128]{2,1,0:T(8,128)(2,1)}, bf16[3,128,128]{2,1,0:T(8,128)(2,1)S(1)}, u32[]{:S(2)}) copy-start(bf16[3,128,128]{2,1,0:T(8,128)(2,1)S(1)} %collective-permute-done.13.refs_2_) | copy-start | bytes 294916
  61.1 13.9 %collective-permute-start.15 = (bf16[3,128,128]{2,1,0:T(8,128)(2,1)}, bf16[3,128,128]{2,1,0:T(8,128)(2,1)S(1)}, u32[]{:S(2)}, u32[]{:S(2)}) collective-permute-start(bf16[3,128,128]{2,1,0:T(8,128)(2,1)} %get-tuple-element.49), channel_id=1, source_target_pairs={{0,5},{1,6},{2,7},{3,8},{4,9},{5,10},{6,11},{7,12},{8,13},{9,14},{... | collective-permute-start | bytes 294920 | tf_op jit(solution)/shard_map/ppermute | solution.py:392
  61.3 10.3 %copy-start.22 = (bf16[112,128]{1,0:T(8,128)(2,1)}, bf16[112,128]{1,0:T(8,128)(2,1)S(1)}, u32[]{:S(2)}) copy-start(bf16[112,128]{1,0:T(8,128)(2,1)S(1)} %collective-permute-done.5.refs_1_) | copy-start | bytes 86020
  61.3 18.6 %collective-permute-start.16 = (bf16[3,128,128]{2,1,0:T(8,128)(2,1)}, bf16[3,128,128]{2,1,0:T(8,128)(2,1)S(1)}, u32[]{:S(2)}, u32[]{:S(2)}) collective-permute-start(bf16[3,128,128]{2,1,0:T(8,128)(2,1)} %get-tuple-element.50), channel_id=1, source_target_pairs={{0,6},{1,7},{2,8},{3,9},{4,10},{5,11},{6,12},{7,13},{8,14},{9,15},... | collective-permute-start | bytes 294920 | tf_op jit(solution)/shard_map/ppermute | solution.py:392
  67.2 4.4 %copy-start.23 = (bf16[112,128]{1,0:T(8,128)(2,1)}, bf16[112,128]{1,0:T(8,128)(2,1)S(1)}, u32[]{:S(2)}) copy-start(bf16[112,128]{1,0:T(8,128)(2,1)S(1)} %collective-permute-done.6.refs_2_) | copy-start | bytes 86020
  67.2 14.5 %collective-permute-start.17 = (bf16[3,128,128]{2,1,0:T(8,128)(2,1)}, bf16[3,128,128]{2,1,0:T(8,128)(2,1)S(1)}, u32[]{:S(2)}, u32[]{:S(2)}) collective-permute-start(bf16[3,128,128]{2,1,0:T(8,128)(2,1)} %get-tuple-element.51), channel_id=1, source_target_pairs={{0,7},{1,8},{2,9},{3,10},{4,11},{5,12},{6,13},{7,14},{8,15},{9,0},... | collective-permute-start | bytes 294920 | tf_op jit(solution)/shard_map/ppermute | solution.py:392
  71.1 12.9 %collective-permute-start.18 = (bf16[3,128,128]{2,1,0:T(8,128)(2,1)}, bf16[3,128,128]{2,1,0:T(8,128)(2,1)S(1)}, u32[]{:S(2)}, u32[]{:S(2)}) collective-permute-start(bf16[3,128,128]{2,1,0:T(8,128)(2,1)} %get-tuple-element.52), channel_id=1, source_target_pairs={{0,8},{1,9},{2,10},{3,11},{4,12},{5,13},{6,14},{7,15},{8,0},{9,1},... | collective-permute-start | bytes 294920 | tf_op jit(solution)/shard_map/ppermute | solution.py:392
  73.1 27.9 %copy-start.7 = (bf16[3,128,128]{2,1,0:T(8,128)(2,1)}, bf16[3,128,128]{2,1,0:T(8,128)(2,1)S(1)}, u32[]{:S(2)}) copy-start(bf16[3,128,128]{2,1,0:T(8,128)(2,1)S(1)} %collective-permute-done.14.refs_3_) | copy-start | bytes 294916
  73.2 14.1 %collective-permute-start.8 = (bf16[4,112,128]{2,1,0:T(8,128)(2,1)}, bf16[4,112,128]{2,1,0:T(8,128)(2,1)S(1)}, u32[]{:S(2)}, u32[]{:S(2)}) collective-permute-start(bf16[4,112,128]{2,1,0:T(8,128)(2,1)} %join.1.refs_0_), channel_id=1, source_target_pairs={{0,2},{1,3},{2,0},{3,1},{4,6},{5,7},{6,4},{7,5},{8,10},{9,11},{10,... | collective-permute-start | bytes 344072 | tf_op jit(solution)/shard_map/ppermute | solution.py:398
  74.9 26.1 %copy-start.8 = (bf16[3,128,128]{2,1,0:T(8,128)(2,1)}, bf16[3,128,128]{2,1,0:T(8,128)(2,1)S(1)}, u32[]{:S(2)}) copy-start(bf16[3,128,128]{2,1,0:T(8,128)(2,1)S(1)} %collective-permute-done.15.refs_4_) | copy-start | bytes 294916
  75.0 12.1 %collective-permute-start.19 = (bf16[3,128,128]{2,1,0:T(8,128)(2,1)S(1)}, bf16[3,128,128]{2,1,0:T(8,128)(2,1)S(1)}, u32[]{:S(2)}, u32[]{:S(2)}) collective-permute-start(bf16[3,128,128]{2,1,0:T(8,128)(2,1)S(1)} %copy-done.28), channel_id=1, source_target_pairs={{0,9},{1,10},{2,11},{3,12},{4,13},{5,14},{6,15},{7,0},{8,1},{9,2},... | collective-permute-start | bytes 294920 | tf_op jit(solution)/shard_map/ppermute | solution.py:392
  79.9 21.2 %copy-start.9 = (bf16[3,128,128]{2,1,0:T(8,128)(2,1)}, bf16[3,128,128]{2,1,0:T(8,128)(2,1)S(1)}, u32[]{:S(2)}) copy-start(bf16[3,128,128]{2,1,0:T(8,128)(2,1)S(1)} %collective-permute-done.16.refs_5_) | copy-start | bytes 294916
  79.9 9.1 %collective-permute-start.20 = (bf16[3,128,128]{2,1,0:T(8,128)(2,1)S(1)}, bf16[3,128,128]{2,1,0:T(8,128)(2,1)S(1)}, u32[]{:S(2)}, u32[]{:S(2)}) collective-permute-start(bf16[3,128,128]{2,1,0:T(8,128)(2,1)S(1)} %copy-done.27), channel_id=1, source_target_pairs={{0,10},{1,11},{2,12},{3,13},{4,14},{5,15},{6,0},{7,1},{8,2},{9,3},... | collective-permute-start | bytes 294920 | tf_op jit(solution)/shard_map/ppermute | solution.py:392
  81.7 19.3 %copy-start.10 = (bf16[3,128,128]{2,1,0:T(8,128)(2,1)}, bf16[3,128,128]{2,1,0:T(8,128)(2,1)S(1)}, u32[]{:S(2)}) copy-start(bf16[3,128,128]{2,1,0:T(8,128)(2,1)S(1)} %collective-permute-done.17.refs_6_) | copy-start | bytes 294916
  81.8 8.7 %collective-permute-start.21 = (bf16[3,128,128]{2,1,0:T(8,128)(2,1)S(1)}, bf16[3,128,128]{2,1,0:T(8,128)(2,1)S(1)}, u32[]{:S(2)}, u32[]{:S(2)}) collective-permute-start(bf16[3,128,128]{2,1,0:T(8,128)(2,1)S(1)} %copy-done.26), channel_id=1, source_target_pairs={{0,11},{1,12},{2,13},{3,14},{4,15},{5,0},{6,1},{7,2},{8,3},{9,4},{... | collective-permute-start | bytes 294920 | tf_op jit(solution)/shard_map/ppermute | solution.py:392
  84.0 17.0 %copy-start.11 = (bf16[3,128,128]{2,1,0:T(8,128)(2,1)}, bf16[3,128,128]{2,1,0:T(8,128)(2,1)S(1)}, u32[]{:S(2)}) copy-start(bf16[3,128,128]{2,1,0:T(8,128)(2,1)S(1)} %collective-permute-done.18.refs_7_) | copy-start | bytes 294916
  84.0 12.0 %collective-permute-start.22 = (bf16[3,128,128]{2,1,0:T(8,128)(2,1)S(1)}, bf16[3,128,128]{2,1,0:T(8,128)(2,1)S(1)}, u32[]{:S(2)}, u32[]{:S(2)}) collective-permute-start(bf16[3,128,128]{2,1,0:T(8,128)(2,1)S(1)} %copy-done.25), channel_id=1, source_target_pairs={{0,12},{1,13},{2,14},{3,15},{4,0},{5,1},{6,2},{7,3},{8,4},{9,5},{1... | collective-permute-start | bytes 294920 | tf_op jit(solution)/shard_map/ppermute | solution.py:392
  87.1 14.0 %copy-start.12 = (bf16[3,128,128]{2,1,0:T(8,128)(2,1)}, bf16[3,128,128]{2,1,0:T(8,128)(2,1)S(1)}, u32[]{:S(2)}) copy-start(bf16[3,128,128]{2,1,0:T(8,128)(2,1)S(1)} %collective-permute-done.19.refs_8_) | copy-start | bytes 294916
  87.1 17.6 %collective-permute-start.9 = (bf16[4,112,128]{2,1,0:T(8,128)(2,1)}, bf16[4,112,128]{2,1,0:T(8,128)(2,1)S(1)}, u32[]{:S(2)}, u32[]{:S(2)}) collective-permute-start(bf16[4,112,128]{2,1,0:T(8,128)(2,1)} %join.1.refs_0_), channel_id=1, source_target_pairs={{0,1},{1,0},{2,3},{3,2},{4,5},{5,4},{6,7},{7,6},{8,9},{9,8},{10,11... | collective-permute-start | bytes 344072 | tf_op jit(solution)/shard_map/ppermute | solution.py:398
  87.3 17.4 %collective-permute-start.10 = (bf16[4,112,128]{2,1,0:T(8,128)(2,1)S(1)}, bf16[4,112,128]{2,1,0:T(8,128)(2,1)S(1)}, u32[]{:S(2)}, u32[]{:S(2)}) collective-permute-start(bf16[4,112,128]{2,1,0:T(8,128)(2,1)S(1)} %collective-permute-done.8.refs_1_), channel_id=1, source_target_pairs={{0,1},{1,0},{2,3},{3,2},{4,5},{5,4},{6,7},{7,6},{8,9},{9,8},{10,11... | collective-permute-start | bytes 344072 | tf_op jit(solution)/shard_map/ppermute | solution.py:398
  88.9 12.1 %copy-start.13 = (bf16[3,128,128]{2,1,0:T(8,128)(2,1)}, bf16[3,128,128]{2,1,0:T(8,128)(2,1)S(1)}, u32[]{:S(2)}) copy-start(bf16[3,128,128]{2,1,0:T(8,128)(2,1)S(1)} %collective-permute-done.20.refs_9_) | copy-start | bytes 294916
  89.0 8.6 %collective-permute-start.23 = (bf16[3,128,128]{2,1,0:T(8,128)(2,1)}, bf16[3,128,128]{2,1,0:T(8,128)(2,1)S(1)}, u32[]{:S(2)}, u32[]{:S(2)}) collective-permute-start(bf16[3,128,128]{2,1,0:T(8,128)(2,1)} %get-tuple-element.57), channel_id=1, source_target_pairs={{0,13},{1,14},{2,15},{3,0},{4,1},{5,2},{6,3},{7,4},{8,5},{9,6},{10... | collective-permute-start | bytes 294920 | tf_op jit(solution)/shard_map/ppermute | solution.py:392
  90.4 10.7 %copy-start.14 = (bf16[3,128,128]{2,1,0:T(8,128)(2,1)}, bf16[3,128,128]{2,1,0:T(8,128)(2,1)S(1)}, u32[]{:S(2)}) copy-start(bf16[3,128,128]{2,1,0:T(8,128)(2,1)S(1)} %collective-permute-done.21.refs_10_) | copy-start | bytes 294916
  90.4 9.1 %collective-permute-start.24 = (bf16[3,128,128]{2,1,0:T(8,128)(2,1)}, bf16[3,128,128]{2,1,0:T(8,128)(2,1)S(1)}, u32[]{:S(2)}, u32[]{:S(2)}) collective-permute-start(bf16[3,128,128]{2,1,0:T(8,128)(2,1)} %get-tuple-element.58), channel_id=1, source_target_pairs={{0,14},{1,15},{2,0},{3,1},{4,2},{5,3},{6,4},{7,5},{8,6},{9,7},{10,... | collective-permute-start | bytes 294920 | tf_op jit(solution)/shard_map/ppermute | solution.py:392
  96.0 5.0 %copy-start.15 = (bf16[3,128,128]{2,1,0:T(8,128)(2,1)}, bf16[3,128,128]{2,1,0:T(8,128)(2,1)S(1)}, u32[]{:S(2)}) copy-start(bf16[3,128,128]{2,1,0:T(8,128)(2,1)S(1)} %collective-permute-done.22.refs_11_) | copy-start | bytes 294916
  96.0 8.7 %copy-start = (bf16[4,112,128]{2,1,0:T(8,128)(2,1)S(1)}, bf16[4,112,128]{2,1,0:T(8,128)(2,1)}, u32[]{:S(2)}) copy-start(bf16[4,112,128]{2,1,0:T(8,128)(2,1)} %join.1.refs_0_) | copy-start | bytes 344068
  96.1 8.7 %copy-start.1 = (f32[2,32,128]{2,1,0:T(8,128)S(1)}, f32[2,32,128]{2,1,0:T(8,128)}, u32[]{:S(2)}) copy-start(f32[2,32,128]{2,1,0:T(8,128)} %get-tuple-element.33.stats_ref) | copy-start | bytes 98308
  96.1 5.0 %collective-permute-start.25 = (bf16[3,128,128]{2,1,0:T(8,128)(2,1)}, bf16[3,128,128]{2,1,0:T(8,128)(2,1)S(1)}, u32[]{:S(2)}, u32[]{:S(2)}) collective-permute-start(bf16[3,128,128]{2,1,0:T(8,128)(2,1)} %get-tuple-element.59), channel_id=1, source_target_pairs={{0,15},{1,0},{2,1},{3,2},{4,3},{5,4},{6,5},{7,6},{8,7},{9,8},{10,9... | collective-permute-start | bytes 294920 | tf_op jit(solution)/shard_map/ppermute | solution.py:392
  (8 other events, 9.0 us)
where the time goes:
time: 110 us; the launch traced here: 109 us
  starting transfers between devices  46.9 us (43%)
  waiting for transfers between devices  34.2 us (31%)
  Pallas kernels  23.8 us (22%)
  local copies, waits for them, and re-layouts  2.75 us (2%)
    ppermute x15, starting transfers between devices, local(): lax.ppermute(bufs[offset - 1], 'ctx', [(i, (i + offset) % devices) for i...  29.9 us
    ppermute x11, waiting for transfers between devices, flip(): return lax.ppermute(x, 'ctx', [(i, i ^ bits) for i in range(devices)])  23.3 us
    ppermute x15, waiting for transfers between devices, local(): lax.ppermute(bufs[offset - 1], 'ctx', [(i, (i + offset) % devices) for i...  10.9 us
    ppermute x11, starting transfers between devices, flip(): return lax.ppermute(x, 'ctx', [(i, i ^ bits) for i in range(devices)])  9.59 us
    all_to_all x1, starting transfers between devices, local(): lax.all_to_all(keys_out, 'ctx', split_axis=0, concat_axis=0, tiled=True)  7.44 us
    pallas_call x1, Pallas kernels, local(): pl.pallas_call(functools.partial(attend_kernel, devices, group, levels),...  6.45 us
    pallas_call x1, Pallas kernels, local(): pl.pallas_call(functools.partial(stage_kernel, devices, group), out_shape...  3.13 us
    pallas_call x1, Pallas kernels, local(): pl.pallas_call(functools.partial(place_values_kernel, devices, group), ou...  2.96 us
  transfers between devices with their start and end apart: 27, of which 10 were waited for; matrix products, arithmetic and copies ran while one was open for 0% of the time, Pallas kernels for 16%

commit v1 on v0

v1 whole, which is shorter than its diff:
```python
import functools

import jax
import jax.numpy as jnp
from jax import lax
from jax.experimental import pallas as pl
from jax.experimental.pallas import tpu as pltpu
from jax.sharding import PartitionSpec as P

absent_score = -1e30
LANES = 128
F32 = jnp.float32
BF16 = jnp.bfloat16
VMEM = pl.BlockSpec(memory_space=pltpu.VMEM)
SMEM = pl.BlockSpec(memory_space=pltpu.SMEM)
HBM = pl.BlockSpec(memory_space=pltpu.HBM)
PARAMS = pltpu.CompilerParams(vmem_limit_bytes=16 * 1024 * 1024)
WHOLE = pltpu.CompilerParams(vmem_limit_bytes=62 * 1024 * 1024)


COST = pl.CostEstimate(flops=1000, bytes_accessed=1000, transcendentals=0)


def stage_kernel(devices, group, me_ref, dest_hbm, k_ref, v_ref, buf, table, k_vm, v_vm, dest, counts, sem, load_sem):
    rows, heads = k_ref.shape[:2]
    small = pltpu.make_async_copy(dest_hbm, dest, sem.at[0])
    small.start()
    loads = []
    for row in range(rows):
        for which, (src, dst) in enumerate(((k_ref, k_vm), (v_ref, v_vm))):
            copy = pltpu.make_async_copy(src.at[row], dst.at[row], load_sem.at[which, row])
            copy.start()
            loads.append(copy)
    me = me_ref[0]

    def clear(i, carry):
        counts[i] = 0
        for k in range(group):
            table[i * group + k] = -1
        return carry

    lax.fori_loop(0, devices, clear, 0)
    small.wait()
    for row in range(rows):
        loads[2 * row].wait()
        loads[2 * row + 1].wait()

        def send(head, carry):
            offset = lax.rem(dest[row, head, 0], devices)
            rank = jnp.minimum(counts[offset], group - 1)
            counts[offset] = rank + 1
            table[offset * group + rank] = row * heads + head
            slot = lax.rem(me + offset, devices) * group + rank
            pltpu.make_async_copy(k_vm.at[row, head], buf.at[slot, 0], sem.at[1]).start()
            pltpu.make_async_copy(v_vm.at[row, head], buf.at[slot, 1], sem.at[2]).start()
            return carry

        lax.fori_loop(0, heads, send, 0)
    pltpu.make_async_copy(k_ref, k_vm, sem.at[1]).wait()
    pltpu.make_async_copy(v_ref, v_vm, sem.at[2]).wait()


def attend_kernel(
    levels,
    me_ref, table, len_hbm, kept_hbm, q_hbm, k_ref, v_ref,
    stats_ref, *rest,
):
    chunks = rest[:levels // 2]
    q_vm, k_vm, v_vm, work, len_ref, kept_ref, load_sem, small_sem, out_sem = rest[levels // 2:]
    rows, heads, tile, width = k_ref.shape
    steps, _, q_heads, _ = q_hbm.shape
    per = q_heads // heads
    me = me_ref[0]

    small = [
        pltpu.make_async_copy(len_hbm, len_ref, small_sem.at[0]),
        pltpu.make_async_copy(kept_hbm, kept_ref, small_sem.at[1]),
    ]
    for copy in small:
        copy.start()
    loads = []
    for row in range(rows):
        copies = [
            pltpu.make_async_copy(q_hbm.at[:, row], q_vm.at[row], load_sem.at[0, row]),
            pltpu.make_async_copy(k_ref.at[row], k_vm.at[row], load_sem.at[1, row]),
            pltpu.make_async_copy(v_ref.at[row], v_vm.at[row], load_sem.at[2, row]),
        ]
        for copy in copies:
            copy.start()
        loads.append(copies)
    for copy in small:
        copy.wait()

    lane = lax.broadcasted_iota(jnp.int32, (per, tile), 1)
    pair_lane = lax.broadcasted_iota(jnp.int32, (steps * per, LANES), 1)
    peaks = jnp.full((steps * per, LANES), absent_score, F32)
    totals = jnp.zeros((steps * per, LANES), F32)
    order = [jnp.bitwise_xor(place_of(me), level) for level in range(levels)]
    scale = width ** -0.5
    block = steps * per
    for row in range(rows):
        for copy in loads[row]:
            copy.wait()
        queries = [q_vm[row, step].astype(F32) for step in order]
        live = []
        for step in order:
            limit = jnp.where(kept_ref[row, step, me] > 0, len_ref[row] - me * tile, 0)
            live.append(lane < limit)
        live = jnp.concatenate(live * heads, axis=0)
        scores = []
        for head in range(heads):
            q = jnp.concatenate([x[head * per:(head + 1) * per] for x in queries], axis=0).astype(BF16)
            scores.append(lax.dot_general(
                q, k_vm[row, head], (((1,), (1,)), ((), ())), preferred_element_type=F32
            ))
        scores = jnp.concatenate(scores, axis=0) * scale
        peak = jnp.max(jnp.where(live, scores, absent_score), axis=1, keepdims=True)
        weights = jnp.where(live, jnp.exp(scores - peak), 0.0)
        total = jnp.sum(weights, axis=1, keepdims=True)
        rounded = weights.astype(BF16)
        for head in range(heads):
            out = jnp.dot(
                rounded[head * block:(head + 1) * block], v_vm[row, head], preferred_element_type=F32
            )
            pair = row * heads + head
            for i in range(levels):
                work[i, pair * per:(pair + 1) * per, :] = out[i * per:(i + 1) * per]
            here = pair_lane == pair
            peaks = jnp.where(here, peak[head * block:(head + 1) * block], peaks)
            totals = jnp.where(here, total[head * block:(head + 1) * block], totals)
    base = rows * q_heads
    for i in range(levels):
        work[i, base:base + per, :] = peaks[i * per:(i + 1) * per]
        work[i, base + per:base + 2 * per, :] = totals[i * per:(i + 1) * per]
    stats_ref[0] = peaks
    stats_ref[1] = totals
    copies = [
        pltpu.make_async_copy(work.at[pl.ds(2 * i, 2)], chunks[i], out_sem.at[i]) for i in range(levels // 2)
    ]
    for copy in copies:
        copy.start()
    for copy in copies:
        copy.wait()


def place_of(me):
    return lax.rem(me, 2) * 2 + lax.rem(me // 2, 2)


def merge(swap, own, got, pairs, per):
    def both(rows):
        x, y = own[rows, :], got[rows, :]
        return jnp.where(swap, y, x), jnp.where(swap, x, y)

    base = pairs * per
    peaks = both(slice(base, base + per))
    totals = both(slice(base + per, base + 2 * per))
    peak = jnp.maximum(*peaks)
    factors = [jnp.exp(x - peak) for x in peaks]
    total = factors[0] * totals[0] + factors[1] * totals[1]

    def summed(pair):
        first, second = [jnp.broadcast_to(f[:, pair:pair + 1], (per, LANES)) for f in factors]
        x, y = both(slice(pair * per, (pair + 1) * per))
        return first * x + second * y

    return peak, total, summed


def merge_kernel(bit, pairs, per, me_ref, own, got, *outs):
    swap = lax.rem(me_ref[0] // bit, 2) == 1
    base = pairs * per
    for i, out in enumerate(outs):
        x, y = (own, got) if len(outs) == 1 else (own.at[i], got.at[i])
        peak, total, summed = merge(swap, x, y, pairs, per)
        for pair in range(pairs):
            out[pair * per:(pair + 1) * per, :] = summed(pair)
        out[base:base + per, :] = peak
        out[base + per:base + 2 * per, :] = total


def last_kernel(bit, pairs, per, me_ref, own, got, out):
    swap = lax.rem(me_ref[0] // bit, 2) == 1
    base = pairs * per
    peak, total, summed = merge(swap, own, got, pairs, per)
    lane = lax.broadcasted_iota(jnp.int32, peak.shape, 1)
    total = jnp.where(lane < pairs, total, 1.0)
    peak = jnp.where(lane < pairs, peak, 0.0)

    def result(pair):
        return summed(pair) / jnp.broadcast_to(total[:, pair:pair + 1], (per, LANES))

    for pair in range(0, pairs, 2):
        both = jnp.concatenate([result(pair), result(pair + 1)], axis=0)
        out[pair * per:(pair + 2) * per, :] = both.astype(BF16)
    rest = jnp.concatenate([peak, total], axis=0)
    lane = lax.broadcasted_iota(jnp.int32, rest.shape, 1)
    parts = []
    for i in range(3):
        parts.append(rest.astype(BF16).astype(F32))
        rest = rest - parts[i]
    half = LANES // 2
    packed = jnp.where(lane < half, parts[0], pltpu.roll(parts[1], half, 1))
    out[base:base + 2 * per, :] = packed.astype(BF16)
    out[base + 2 * per:base + 4 * per, :] = parts[2].astype(BF16)


def finish_kernel(pairs, per, heads, levels, me_ref, stats_ref, *refs):
    ins, out, mass_ref = refs[:levels], refs[levels], refs[levels + 1]
    base = pairs * per
    lane = lax.broadcasted_iota(jnp.int32, (2 * per, LANES), 1)
    mass = jnp.zeros((per, LANES), F32)
    for level in range(levels):
        step = jnp.bitwise_xor(place_of(me_ref[0]), level)
        out[step] = ins[level][:base, :]
        packed = ins[level][base:base + 2 * per, :].astype(F32)
        third = ins[level][base + 2 * per:base + 4 * per, :].astype(F32)
        both = third + pltpu.roll(packed, LANES // 2, 1) + packed
        both = jnp.where(lane < pairs, both, 1.0)
        at = level * per
        coefficient = jnp.exp(jnp.minimum(stats_ref[0, at:at + per, :] - both[:per], 0.0)) / both[per:]
        mass = mass + stats_ref[1, at:at + per, :] * coefficient
    mass = jnp.sum(mass, axis=0, keepdims=True)
    for row in range(pairs // heads):
        mass_ref[row] = mass[:, row * heads:(row + 1) * heads]


def place_kernel(devices, group, me_ref, table, got_ref, k_ref, v_ref, me_out, got_vm, sem, load_sem):
    heads = k_ref.shape[1]
    me = me_ref[0]
    me_out[0] = me
    loads = []
    for offset in range(devices):
        source = lax.rem(me + devices - offset, devices)
        part = got_ref.at[pl.ds(source * group, group)]
        copy = pltpu.make_async_copy(part, got_vm.at[pl.ds(offset * group, group)], load_sem.at[offset])
        copy.start()
        loads.append(copy)
    for offset in range(devices):
        loads[offset].wait()
        for slot in range(offset * group, (offset + 1) * group):
            pair = table[slot]

            @pl.when(pair >= 0)
            def _():
                row, head = pair // heads, lax.rem(pair, heads)
                for which, ref in enumerate((k_ref, v_ref)):
                    pltpu.make_async_copy(got_vm.at[slot, which], ref.at[row, head], sem.at[which]).start()
    pltpu.make_async_copy(k_ref, k_ref, sem.at[0]).wait()
    pltpu.make_async_copy(v_ref, v_ref, sem.at[1]).wait()


def local(queries, key_cache, value_cache, row_lengths, kept_tiles, tile_dest):
    devices = lax.axis_size("ctx")
    rows, heads, span, width = key_cache.shape
    steps, _, q_heads, _ = queries.shape
    per = q_heads // heads
    pairs = rows * heads
    group = -(-pairs // devices)
    levels = 4
    assert steps == levels and tile_dest.shape[2] == devices and pairs % 2 == 0 and pairs <= LANES // 2
    assert devices > levels and devices & (devices - 1) == 0 and width == LANES

    me = lax.axis_index("ctx").astype(jnp.int32).reshape(1)
    kept = jnp.transpose(kept_tiles, (1, 0, 2))
    block_rows = rows * q_heads + 2 * per
    block_type = jax.ShapeDtypeStruct((block_rows, width), F32)
    message_type = jax.ShapeDtypeStruct((rows * q_heads + 4 * per, width), BF16)
    tiles_type = jax.ShapeDtypeStruct((devices * group, 2, span, width), BF16)

    tiles_out, table = pl.pallas_call(
        functools.partial(stage_kernel, devices, group),
        out_shape=[tiles_type, jax.ShapeDtypeStruct((devices * group,), jnp.int32)],
        in_specs=[SMEM, HBM, HBM, HBM],
        out_specs=[HBM, SMEM],
        scratch_shapes=[
            pltpu.VMEM(key_cache.shape, BF16),
            pltpu.VMEM(value_cache.shape, BF16),
            pltpu.SMEM(tile_dest.shape, jnp.int32),
            pltpu.SMEM((devices,), jnp.int32),
            pltpu.SemaphoreType.DMA((3,)),
            pltpu.SemaphoreType.DMA((2, rows)),
        ],
        compiler_params=WHOLE,
        cost_estimate=COST,
        name="stage",
    )(me, tile_dest, key_cache, value_cache)
    tiles_in = lax.all_to_all(tiles_out, "ctx", split_axis=0, concat_axis=0, tiled=True)

    stats, *chunks = pl.pallas_call(
        functools.partial(attend_kernel, levels),
        out_shape=[
            jax.ShapeDtypeStruct((2, steps * per, LANES), F32),
        ] + [jax.ShapeDtypeStruct((2, block_rows, width), F32)] * 2,
        in_specs=[SMEM, SMEM, HBM, HBM, HBM, HBM, HBM],
        out_specs=[VMEM] + [HBM] * 2,
        scratch_shapes=[
            pltpu.VMEM((rows, steps, q_heads, width), BF16),
            pltpu.VMEM(key_cache.shape, BF16),
            pltpu.VMEM(value_cache.shape, BF16),
            pltpu.VMEM((levels, block_rows, width), F32),
            pltpu.SMEM(row_lengths.shape, jnp.int32),
            pltpu.SMEM(kept.shape, jnp.int32),
            pltpu.SemaphoreType.DMA((3, rows)),
            pltpu.SemaphoreType.DMA((2,)),
            pltpu.SemaphoreType.DMA((2,)),
        ],
        compiler_params=WHOLE,
        cost_estimate=COST,
        name="attend",
    )(me, table, row_lengths, kept, queries, key_cache, value_cache)

    def flip(x, bit):
        return lax.ppermute(x, "ctx", [(i, i ^ bit) for i in range(devices)])

    def merged(kernel, name, bit, own, got, out_shape):
        return pl.pallas_call(
            functools.partial(kernel, bit, pairs, per),
            out_shape=out_shape,
            in_specs=[SMEM, VMEM, VMEM],
            out_specs=[VMEM] * len(out_shape),
            compiler_params=PARAMS,
            cost_estimate=COST,
            name=name,
        )(me, own, got)

    block, sent = merged(merge_kernel, "core", 1, chunks[0], flip(chunks[1], 1), [block_type] * 2)
    block, = merged(merge_kernel, "near", 2, block, flip(sent, 2), [block_type])
    bit = levels
    while 2 * bit < devices:
        block, = merged(merge_kernel, "far", bit, block, flip(block, bit), [block_type])
        bit *= 2
    message, = merged(last_kernel, "last", bit, block, flip(block, bit), [message_type])
    other = flip(message, 2)

    moved_keys, moved_values, me_next = pl.pallas_call(
        functools.partial(place_kernel, devices, group),
        out_shape=[
            jax.ShapeDtypeStruct(key_cache.shape, BF16),
            jax.ShapeDtypeStruct(value_cache.shape, BF16),
            jax.ShapeDtypeStruct((1,), jnp.int32),
        ],
        in_specs=[SMEM, SMEM, HBM],
        out_specs=[HBM, HBM, SMEM],
        scratch_shapes=[
            pltpu.VMEM(tiles_type.shape, BF16),
            pltpu.SemaphoreType.DMA((2,)),
            pltpu.SemaphoreType.DMA((devices,)),
        ],
        compiler_params=WHOLE,
        cost_estimate=COST,
        name="place",
    )(me, table, tiles_in)

    attn_out, mass = pl.pallas_call(
        functools.partial(finish_kernel, pairs, per, heads, levels),
        out_shape=[
            jax.ShapeDtypeStruct((steps, rows * q_heads, width), BF16),
            jax.ShapeDtypeStruct((rows, 1, heads), F32),
        ],
        in_specs=[SMEM, VMEM] + [VMEM] * levels,
        out_specs=[VMEM, VMEM],
        compiler_params=PARAMS,
        cost_estimate=COST,
        name="finish",
    )(me_next, stats, message, other, flip(message, 1), flip(other, 1))
    return attn_out.reshape(queries.shape), jnp.transpose(mass, (0, 2, 1)), moved_keys, moved_values


def solution(mesh):
    in_specs = (
        P(None, "grp", None, None),
        P("grp", None, "ctx", None),
        P("grp", None, "ctx", None),
        P("grp"),
        P(None, "grp", None),
        P("grp", None, None),
    )
    out_specs = (
        P(None, "grp", None, None),
        P("grp", None, "ctx"),
        P("grp", None, "ctx", None),
        P("grp", None, "ctx", None),
    )
    return jax.shard_map(local, mesh=mesh, in_specs=in_specs, out_specs=out_specs, check_vma=False)
```

time: 110 us -> 103 us (0.936); the launches traced: 109 us -> 103 us
  waiting for transfers between devices: 34.2 us -> 68.4 us
  starting transfers between devices: 46.9 us -> 16 us
  Pallas kernels: 23.8 us -> 16.5 us
  local copies, waits for them, and re-layouts: 2.75 us -> 1.01 us
    ppermute x26 -> x7, waiting for transfers between devices: 34.2 us -> 68.4 us  [flip(): return lax.ppermute(x, 'ctx', [(i, i ^ bit) for i in range(devices)])]
    ppermute x26 -> x7, starting transfers between devices: 39.5 us -> 8.58 us  [flip(): return lax.ppermute(x, 'ctx', [(i, i ^ bit) for i in range(devices)])]
    pallas_call x8 -> x7, Pallas kernels: 20.7 us -> 13 us  [the longest x1 6.19 us: local(): pl.pallas_call(functools.partial(attend_kernel, levels), out_shape=[jax.S...]
    unnamed x58 -> x4, local copies, waits for them, and re-layouts: 2.75 us -> 1.01 us
  transfers between devices with their start and end apart: 27 -> 8, of which waited for: 10 -> 5; matrix products, arithmetic and copies ran while one was open for 0% -> 0% of each run, Pallas kernels for 16% -> 11%
where the time goes in v1:
time: 103 us
  waiting for transfers between devices  68.4 us (66%)
  Pallas kernels  16.5 us (16%)
  starting transfers between devices  16 us (16%)
    ppermute x7, waiting for transfers between devices, flip(): return lax.ppermute(x, 'ctx', [(i, i ^ bit) for i in range(devices)])  68.4 us
    ppermute x7, starting transfers between devices, flip(): return lax.ppermute(x, 'ctx', [(i, i ^ bit) for i in range(devices)])  8.58 us
    all_to_all x1, starting transfers between devices, local(): lax.all_to_all(tiles_out, 'ctx', split_axis=0, concat_axis=0, tiled=True)  7.45 us
    pallas_call x1, Pallas kernels, local(): pl.pallas_call(functools.partial(attend_kernel, levels), out_shape=[jax.S...  6.19 us
    pallas_call x1, Pallas kernels, local(): pl.pallas_call(functools.partial(place_kernel, devices, group), out_shape...  4.21 us
    pallas_call x1, Pallas kernels, local(): pl.pallas_call(functools.partial(stage_kernel, devices, group), out_shape...  3.52 us
  transfers between devices with their start and end apart: 8, of which 5 were waited for; matrix products, arithmetic and copies ran while one was open for 0% of the time, Pallas kernels for 11%

profile of v1, /device:TPU:0, one launch (start us, length us, event | category | flops | bytes accessed | tf_op | source)
XLA Modules:
  0.0 102.7 jit_solution(4336797267547348940)
XLA Ops:
  0.6 3.5 %stage.1 = (bf16[48,2,128,128]{3,2,1,0:T(8,128)(2,1)}, s32[48]{0:T(128)}) custom-call(s32[1]{0:T(128)} %bitcast.me_ref, s32[6,8,16]{2,1,0:T(8,128)} %dest_hbm.1, bf16[6,8,128,128]{3,2,1,0:T(8,128)(2,1)} %k_ref.3, bf16[6,8,128,128]{3,2,1,0:T(8,128)(2,1)} %v_ref.3), custom_call_target="tpu_custom_call" | custom-call | flops 1000 | bytes 1000 | tf_op jit(solution)/shard_map/stage/pallas_call | solution.py:271
  4.2 7.5 %all-to-all-start = ((bf16[48,2,128,128]{3,2,1,0:T(8,128)(2,1)}), bf16[48,2,128,128]{3,2,1,0:T(8,128)(2,1)}, u32[]{:S(2)}, u32[]{:S(2)}) async-start(bf16[48,2,128,128]{3,2,1,0:T(8,128)(2,1)} %get-tuple-element.17), calls=%async_computation | async-start | bytes 6291456 | tf_op jit(solution)/shard_map/all_to_all | solution.py:288
  11.6 6.2 %attend.1 = (f32[2,32,128]{2,1,0:T(8,128)}, f32[2,400,128]{2,1,0:T(8,128)}, f32[2,400,128]{2,1,0:T(8,128)}) custom-call(s32[1]{0:T(128)} %bitcast.me_ref, s32[48]{0:T(128)} %get-tuple-element.16.table, s32[6]{0:T(128)} %len_hbm.1, s32[6,4,16]{2,1,0:T(4,128)} %bitcast.4, bf16[4,6,64,128]{3,2,1,0:T(8,128)(2,1)} %q_hbm.1, bf16[6,8,128,128]{3,2,1,0:T(8,128)(2,1)} %k_ref.3, ...), custom_call_target="tpu_custom_call" | custom-call | flops 1000 | bytes 1000 | tf_op jit(solution)/shard_map/attend/pallas_call | solution.py:290
  17.8 0.4 collective-permute-start
  18.2 1.6 %collective-permute-done.got = f32[2,400,128]{2,1,0:T(8,128)S(1)} collective-permute-done((f32[2,400,128]{2,1,0:T(8,128)}, f32[2,400,128]{2,1,0:T(8,128)S(1)}, u32[]{:S(2)}, u32[]{:S(2)}) %collective-permute-start) | collective-permute-done | bytes 409632 | tf_op jit(solution)/shard_map/ppermute | solution.py:314
  19.8 0.0 copy-start
  19.8 1.0 copy-done
  20.8 0.4 core.1
  21.2 1.9 %collective-permute-start.1 = (f32[400,128]{1,0:T(8,128)S(1)}, f32[400,128]{1,0:T(8,128)S(1)}, u32[]{:S(2)}, u32[]{:S(2)}) collective-permute-start(f32[400,128]{1,0:T(8,128)S(1)} %get-tuple-element.23), channel_id=1, source_target_pairs={{0,2},{1,3},{2,0},{3,1},{4,6},{5,7},{6,4},{7,5},{8,10},{9,11},{10,... | collective-permute-start | bytes 614408 | tf_op jit(solution)/shard_map/ppermute | solution.py:314
  23.2 13.8 %collective-permute-done.1.got = f32[400,128]{1,0:T(8,128)S(1)} collective-permute-done((f32[400,128]{1,0:T(8,128)S(1)}, f32[400,128]{1,0:T(8,128)S(1)}, u32[]{:S(2)}, u32[]{:S(2)}) %collective-permute-start.1) | collective-permute-done | bytes 204832 | tf_op jit(solution)/shard_map/ppermute | solution.py:314
  37.0 0.2 near.1.own
  37.2 0.1 collective-permute-start.2
  37.3 30.5 %collective-permute-done.2.got = f32[400,128]{1,0:T(8,128)S(1)} collective-permute-done((f32[400,128]{1,0:T(8,128)S(1)}, f32[400,128]{1,0:T(8,128)S(1)}, u32[]{:S(2)}, u32[]{:S(2)}) %collective-permute-start.2) | collective-permute-done | bytes 204832 | tf_op jit(solution)/shard_map/ppermute | solution.py:314
  67.8 0.2 far.1.own
  68.0 4.6 %collective-permute-start.3 = (f32[400,128]{1,0:T(8,128)S(1)}, f32[400,128]{1,0:T(8,128)S(1)}, u32[]{:S(2)}, u32[]{:S(2)}) collective-permute-start(f32[400,128]{1,0:T(8,128)S(1)} %far.1.own), channel_id=1, source_target_pairs={{0,8},{1,9},{2,10},{3,11},{4,12},{5,13},{6,14},{7,15},{8,0},{9,1},... | collective-permute-start | bytes 614408 | tf_op jit(solution)/shard_map/ppermute | solution.py:314
  72.6 19.4 %collective-permute-done.3.got = f32[400,128]{1,0:T(8,128)S(1)} collective-permute-done((f32[400,128]{1,0:T(8,128)S(1)}, f32[400,128]{1,0:T(8,128)S(1)}, u32[]{:S(2)}, u32[]{:S(2)}) %collective-permute-start.3) | collective-permute-done | bytes 204832 | tf_op jit(solution)/shard_map/ppermute | solution.py:314
  91.9 0.3 last.1.refs_0_
  92.3 0.0 copy-start.1
  92.3 1.6 %collective-permute-start.4 = (bf16[416,128]{1,0:T(8,128)(2,1)S(1)}, bf16[416,128]{1,0:T(8,128)(2,1)S(1)}, u32[]{:S(2)}, u32[]{:S(2)}) collective-permute-start(bf16[416,128]{1,0:T(8,128)(2,1)S(1)} %last.1.refs_0_), channel_id=1, source_target_pairs={{0,2},{1,3},{2,0},{3,1},{4,6},{5,7},{6,4},{7,5},{8,10},{9,11},{10,... | collective-permute-start | bytes 319496 | tf_op jit(solution)/shard_map/ppermute | solution.py:314
  93.8 0.0 collective-permute-start.5
  93.8 3.2 %collective-permute-done.4.refs_1_ = bf16[416,128]{1,0:T(8,128)(2,1)S(1)} collective-permute-done((bf16[416,128]{1,0:T(8,128)(2,1)S(1)}, bf16[416,128]{1,0:T(8,128)(2,1)S(1)}, u32[]{:S(2)}, u32[]{:S(2)}) %collective-permute-start.4) | collective-permute-done | bytes 106528 | tf_op jit(solution)/shard_map/ppermute | solution.py:314
  97.0 0.0 collective-permute-start.6
  97.0 0.0 all-to-all-done.got_ref
  97.0 4.2 %place.1 = (bf16[6,8,128,128]{3,2,1,0:T(8,128)(2,1)}, bf16[6,8,128,128]{3,2,1,0:T(8,128)(2,1)}, s32[1]{0:T(128)}) custom-call(s32[1]{0:T(128)} %bitcast.me_ref, s32[48]{0:T(128)} %get-tuple-element.16.table, bf16[48,2,128,128]{3,2,1,0:T(8,128)(2,1)} %all-to-all-done.got_ref), custom_call_target="tpu_custom_call" | custom-call | flops 1000 | bytes 1000 | tf_op jit(solution)/shard_map/place/pallas_call | solution.py:336
  101.3 0.0 collective-permute-done.5.refs_2_
  101.3 0.0 collective-permute-done.6.refs_3_
  101.3 0.0 copy-done.1
  101.3 1.4 %finish.1 = (bf16[4,384,128]{2,1,0:T(8,128)(2,1)}, f32[6,1,8]{2,1,0:T(1,128)}) custom-call(s32[1]{0:T(128)} %get-tuple-element.18.me_ref, f32[2,32,128]{2,1,0:T(8,128)S(1)} %copy-done.1, bf16[416,128]{1,0:T(8,128)(2,1)S(1)} %last.1.refs_0_, bf16[416,128]{1,0:T(8,128)(2,1)S(1)} %collective-permute-done.4.refs_1_, ...), custom_call_target="tpu_custom_call" | custom-call | flops 1000 | bytes 1000 | tf_op jit(solution)/shard_map/finish/pallas_call | solution.py:355
Async XLA Ops:
  4.2 92.9 %all-to-all-start = ((bf16[48,2,128,128]{3,2,1,0:T(8,128)(2,1)}), bf16[48,2,128,128]{3,2,1,0:T(8,128)(2,1)}, u32[]{:S(2)}, u32[]{:S(2)}) async-start(bf16[48,2,128,128]{3,2,1,0:T(8,128)(2,1)} %get-tuple-element.17), calls=%async_computation | async-start | bytes 6291456 | tf_op jit(solution)/shard_map/all_to_all | solution.py:288
  17.8 2.0 %collective-permute-start = (f32[2,400,128]{2,1,0:T(8,128)}, f32[2,400,128]{2,1,0:T(8,128)S(1)}, u32[]{:S(2)}, u32[]{:S(2)}) collective-permute-start(f32[2,400,128]{2,1,0:T(8,128)} %get-tuple-element.21), channel_id=1, source_target_pairs={{0,1},{1,0},{2,3},{3,2},{4,5},{5,4},{6,7},{7,6},{8,9},{9,8},{10,11... | collective-permute-start | bytes 1228808 | tf_op jit(solution)/shard_map/ppermute | solution.py:314
  19.8 1.0 copy-start
  21.2 15.7 %collective-permute-start.1 = (f32[400,128]{1,0:T(8,128)S(1)}, f32[400,128]{1,0:T(8,128)S(1)}, u32[]{:S(2)}, u32[]{:S(2)}) collective-permute-start(f32[400,128]{1,0:T(8,128)S(1)} %get-tuple-element.23), channel_id=1, source_target_pairs={{0,2},{1,3},{2,0},{3,1},{4,6},{5,7},{6,4},{7,5},{8,10},{9,11},{10,... | collective-permute-start | bytes 614408 | tf_op jit(solution)/shard_map/ppermute | solution.py:314
  37.2 30.6 %collective-permute-start.2 = (f32[400,128]{1,0:T(8,128)S(1)}, f32[400,128]{1,0:T(8,128)S(1)}, u32[]{:S(2)}, u32[]{:S(2)}) collective-permute-start(f32[400,128]{1,0:T(8,128)S(1)} %near.1.own), channel_id=1, source_target_pairs={{0,4},{1,5},{2,6},{3,7},{4,0},{5,1},{6,2},{7,3},{8,12},{9,13},{10,... | collective-permute-start | bytes 614408 | tf_op jit(solution)/shard_map/ppermute | solution.py:314
  68.0 23.9 %collective-permute-start.3 = (f32[400,128]{1,0:T(8,128)S(1)}, f32[400,128]{1,0:T(8,128)S(1)}, u32[]{:S(2)}, u32[]{:S(2)}) collective-permute-start(f32[400,128]{1,0:T(8,128)S(1)} %far.1.own), channel_id=1, source_target_pairs={{0,8},{1,9},{2,10},{3,11},{4,12},{5,13},{6,14},{7,15},{8,0},{9,1},... | collective-permute-start | bytes 614408 | tf_op jit(solution)/shard_map/ppermute | solution.py:314
  92.3 9.0 %copy-start.1 = (f32[2,32,128]{2,1,0:T(8,128)S(1)}, f32[2,32,128]{2,1,0:T(8,128)}, u32[]{:S(2)}) copy-start(f32[2,32,128]{2,1,0:T(8,128)} %get-tuple-element.19.stats_ref) | copy-start | bytes 98308
  92.3 4.8 %collective-permute-start.4 = (bf16[416,128]{1,0:T(8,128)(2,1)S(1)}, bf16[416,128]{1,0:T(8,128)(2,1)S(1)}, u32[]{:S(2)}, u32[]{:S(2)}) collective-permute-start(bf16[416,128]{1,0:T(8,128)(2,1)S(1)} %last.1.refs_0_), channel_id=1, source_target_pairs={{0,2},{1,3},{2,0},{3,1},{4,6},{5,7},{6,4},{7,5},{8,10},{9,11},{10,... | collective-permute-start | bytes 319496 | tf_op jit(solution)/shard_map/ppermute | solution.py:314
  93.8 7.4 %collective-permute-start.5 = (bf16[416,128]{1,0:T(8,128)(2,1)S(1)}, bf16[416,128]{1,0:T(8,128)(2,1)S(1)}, u32[]{:S(2)}, u32[]{:S(2)}) collective-permute-start(bf16[416,128]{1,0:T(8,128)(2,1)S(1)} %last.1.refs_0_), channel_id=1, source_target_pairs={{0,1},{1,0},{2,3},{3,2},{4,5},{5,4},{6,7},{7,6},{8,9},{9,8},{10,11... | collective-permute-start | bytes 319496 | tf_op jit(solution)/shard_map/ppermute | solution.py:314
  97.0 4.2 %collective-permute-start.6 = (bf16[416,128]{1,0:T(8,128)(2,1)S(1)}, bf16[416,128]{1,0:T(8,128)(2,1)S(1)}, u32[]{:S(2)}, u32[]{:S(2)}) collective-permute-start(bf16[416,128]{1,0:T(8,128)(2,1)S(1)} %collective-permute-done.4.refs_1_), channel_id=1, source_target_pairs={{0,1},{1,0},{2,3},{3,2},{4,5},{5,4},{6,7},{7,6},{8,9},{9,8},{10,11... | collective-permute-start | bytes 319496 | tf_op jit(solution)/shard_map/ppermute | solution.py:314
